TPU v7x, 256 devices: a whole 4x4x8 slice. The times are simulated.
256 devices in a mesh: tm: 8 (over y_hi, x), space: 32 (over z, y_lo, core).
Axes of the slice: x: 4, y: 4 (y_hi: 2, y_lo: 2; y = y_hi * 2 + y_lo), z: 8, core: 2. Of those that a mesh axis runs over, the one named last changes fastest.
Arguments:
- vectors: float32 [8, 2, 3, 64, 8192], P('tm', None, None, None, 'space'), may hold values from -6 to 6
- perambulators: float32 [8, 16, 2, 4096], P('tm'), may hold values from -0.75 to 0.75
- shift_steps: int32 [8], P('tm'), may hold values from 1 to 7, as said below
- spin_choice: int32 [4, 3], replicated, may hold values from 0 to 15
Outputs:
- elementals: float32 [8, 64, 2, 4096], P('tm', 'space')
- correlator: float32 [8, 4, 2], P('tm')
Inputs may be any that keep to these rules, and one draw needn't show every extreme that they name: `shift_steps`: every distance from 1 to 7 is taken by at least one source timeslice. `spin_choice`: each entry is alpha 4 + beta for a pair of spin indices.
All inputs are finite; a program needn't handle non-finite values.
Results may differ from a plain program's by a relative error of at most 0.0003.
Values sent between devices are 32-bit elements; how exact they have to be, the bound alone decides.
No kernel may reach another device: no remote copies, remote signals or barrier semaphores. Data moves between devices by JAX's collectives and lax.ppermute only.
A program may use at most 64 MiB of HBM per device.

v0:
```python
import math

import jax
import jax.numpy as jnp
from jax import lax
from jax.sharding import PartitionSpec as P

exact_mode = lax.Precision.HIGHEST


def complex_product(left_re, left_im, right_re, right_im):
    return (left_re * right_re - left_im * right_im, left_re * right_im + left_im * right_re)


def rotate(values, places):
    return jnp.concatenate([values[places:], values[:places]], axis=0)


def contract_first(left, right):
    return lax.dot_general(left, right, (((0,), (0,)), ((), ())), precision=exact_mode)


def inner_rows(left, right):
    return lax.dot_general(left, right, (((1,), (1,)), ((), ())), precision=exact_mode)


def complex_einsum(form, left, right):
    first = jnp.einsum(form, left[0], right[0], precision=exact_mode) - jnp.einsum(
        form, left[1], right[1], precision=exact_mode
    )
    second = jnp.einsum(form, left[0], right[1], precision=exact_mode) + jnp.einsum(
        form, left[1], right[0], precision=exact_mode
    )
    return (first, second)


def elemental_rows(vec_re, vec_im, lead_re, lead_im, first_row, row_count, factor):
    sites = vec_re.shape[1]
    nvec = vec_re.shape[2]
    block = math.gcd(row_count, 4)

    def one_block(index):
        offset = first_row + index * block
        part_re = lax.dynamic_slice_in_dim(vec_re, offset, block, 2)[:, :, :, None]
        part_im = lax.dynamic_slice_in_dim(vec_im, offset, block, 2)[:, :, :, None]
        full_re = vec_re[:, :, None, :]
        full_im = vec_im[:, :, None, :]
        one_re, one_im = complex_product(
            rotate(part_re, 1), rotate(part_im, 1), rotate(full_re, 2), rotate(full_im, 2)
        )
        two_re, two_im = complex_product(
            rotate(part_re, 2), rotate(part_im, 2), rotate(full_re, 1), rotate(full_im, 1)
        )
        cross_re = (one_re - two_re).reshape(3 * sites, block * nvec)
        cross_im = (one_im - two_im).reshape(3 * sites, block * nvec)
        out_re = contract_first(lead_re, cross_re) - contract_first(lead_im, cross_im)
        out_im = contract_first(lead_re, cross_im) + contract_first(lead_im, cross_re)
        stacked = jnp.stack([out_re, out_im], 0).reshape(2, nvec, block, nvec)
        return jnp.transpose(stacked, (2, 0, 1, 3)).reshape(block, 2, nvec * nvec) * factor

    result = lax.map(one_block, jnp.arange(row_count // block, dtype=jnp.int32))
    return result.reshape(row_count, 2, nvec * nvec)


def transform_rows(own, mats, nvec):
    combos = mats.shape[0]
    row_count = own.shape[0]
    elem = (own[:, 0].reshape(row_count, nvec, nvec), own[:, 1].reshape(row_count, nvec, nvec))
    first_mat = (
        mats[:, 0, 0].reshape(combos, nvec, nvec),
        mats[:, 0, 1].reshape(combos, nvec, nvec),
    )
    third_mat = (
        mats[:, 2, 0].reshape(combos, nvec, nvec),
        mats[:, 2, 1].reshape(combos, nvec, nvec),
    )
    half = complex_einsum("jik,slk->sjil", elem, third_mat)
    done = complex_einsum("smi,sjil->sjml", first_mat, half)
    return (
        done[0].reshape(combos * row_count, nvec * nvec),
        done[1].reshape(combos * row_count, nvec * nvec),
    )


def pair_sum(sink_rows, trans_re, trans_im, mid_re, mid_im):
    combos = mid_re.shape[0]
    sink_count = sink_rows.shape[0]
    own_count = mid_re.shape[2]
    sink_re = sink_rows[:, 0]
    sink_im = sink_rows[:, 1]
    inner_re = (inner_rows(sink_re, trans_re) + inner_rows(sink_im, trans_im)).reshape(
        sink_count, combos, own_count
    )
    inner_im = (inner_rows(sink_re, trans_im) - inner_rows(sink_im, trans_re)).reshape(
        sink_count, combos, own_count
    )
    total_re = jnp.einsum("srj,rsj->s", mid_re, inner_re, precision=exact_mode) - jnp.einsum(
        "srj,rsj->s", mid_im, inner_im, precision=exact_mode
    )
    total_im = jnp.einsum("srj,rsj->s", mid_re, inner_im, precision=exact_mode) + jnp.einsum(
        "srj,rsj->s", mid_im, inner_re, precision=exact_mode
    )
    return jnp.stack([total_re, total_im], -1)


def shards(vectors, perambulators, shift_steps, spin_choice):
    local_vec = vectors[0]
    nvec = local_vec.shape[2]
    sites = local_vec.shape[3]
    space_count = lax.axis_size("space")
    time_count = lax.axis_size("tm")
    vec_re = jnp.transpose(local_vec[0], (0, 2, 1))
    vec_im = jnp.transpose(local_vec[1], (0, 2, 1))
    lead_re = vec_re.reshape(3 * sites, nvec)
    lead_im = vec_im.reshape(3 * sites, nvec)
    factor = 1.0 / math.sqrt(24.0 * sites * space_count)
    corr_factor = 0.25 / (nvec * math.sqrt(nvec))
    own_count = nvec // space_count
    own_first = lax.axis_index("space") * own_count
    summed = lax.psum(elemental_rows(vec_re, vec_im, lead_re, lead_im, 0, nvec, factor), "space")
    own = lax.dynamic_slice_in_dim(summed, own_first, own_count, 0)
    every_time = lax.all_gather(own[None], "tm", axis=0, tiled=True)
    target = (lax.axis_index("tm") + shift_steps[0]) % time_count
    sink = lax.dynamic_index_in_dim(every_time, target, 0, keepdims=False)
    combos = spin_choice.shape[0]
    spin_pairs = perambulators.shape[1]
    one_hot = (
        spin_choice[:, :, None] == jnp.arange(spin_pairs, dtype=jnp.int32)[None, None, :]
    ).astype(jnp.float32)
    mats = jnp.einsum("sqm,mcf->sqcf", one_hot, perambulators[0], precision=exact_mode)
    trans_re, trans_im = transform_rows(own, mats, nvec)
    mid_re = lax.dynamic_slice_in_dim(
        mats[:, 1, 0].reshape(combos, nvec, nvec), own_first, own_count, 2
    )
    mid_im = lax.dynamic_slice_in_dim(
        mats[:, 1, 1].reshape(combos, nvec, nvec), own_first, own_count, 2
    )
    sink_rows = lax.all_gather(sink, "space", axis=0, tiled=True)
    partial_corr = pair_sum(sink_rows, trans_re, trans_im, mid_re, mid_im)
    correlator = lax.psum(partial_corr, "space") * corr_factor
    return (own[None], correlator[None])


def solution(mesh):
    placed = (P("tm", None, None, None, "space"), P("tm", None, None, None), P("tm"), P())
    return jax.shard_map(
        shards,
        mesh=mesh,
        in_specs=placed,
        out_specs=(P("tm", "space", None, None), P("tm", None, None)),
        check_vma=False,
    )
```

profile of v0, /device:TPU:1, one launch (start us, length us, event | category | flops | bytes accessed | tf_op | source)
XLA Modules:
  0.0 586.6 jit_solution(3519900999128513258)
XLA Ops:
  16.7 161.8 %while.11 = (s32[]{:T(128)}, f32[16,4,2,4096]{3,2,1,0:T(2,128)}, s32[16]{0:T(128)S(1)}, f32[3,256,64]{1,0,2:T(4,128)}, f32[3,256,1,64]{1,0,3,2:T(4,128)S(1)}, /*...) while((s32[]{:T(128)}, f32[16,4,2,4096]{3,2,1,0:T(2,128)}, ...), condition=%wide.region_1.2_spmd, body=%wide.region_0.1_spmd.sunk | while | flops 606842880 | bytes 11387647 | solution.py:61
  21.8 1.4 fusion.85
  31.9 1.4 fusion.85
  42.0 1.4 fusion.85
  52.1 1.4 fusion.85
  62.2 1.4 fusion.85
  72.4 1.4 fusion.85
  82.5 1.4 fusion.85
  92.6 1.4 fusion.85
  102.7 1.4 fusion.85
  112.8 1.4 fusion.85
  122.9 1.4 fusion.85
  133.1 1.4 fusion.85
  153.3 1.4 fusion.85
  179.3 233.6 %all-reduce.2.cloned.1.call-done = f32[64,2,4096]{2,1,0:T(2,128)} async-done(((f32[64,2,4096]{2,1,0:T(2,128)}), f32[64,2,4096]{2,1,0:T(2,128)}) %all-reduce.2.cloned.1.call-update) | async-done | bytes 2097168 | tf_op jit(solution)/shard_map/psum | solution.py:120
  413.8 29.2 %all-gather = f32[16,2,4096]{2,1,0:T(2,128)S(1)} all-gather(f32[2,2,4096]{2,1,0:T(2,128)S(1)} %constant_dynamic-slice_fusion), channel_id=2, replica_groups=mesh['tm'=8,'space'=32] {'tm'}, dimensions={0}, use_global_device_ids=true | all-gather | bytes 589824 | tf_op jit(solution)/shard_map/all_gather | solution.py:122
  450.7 64.0 %all-gather.4.cloned.1.call-done = f32[1,64,2,4096]{3,2,0,1:T(2,128)} async-done(((f32[1,2,2,4096]{3,2,0,1:T(2,128)}), f32[1,64,2,4096]{3,2,0,1:T(2,128)}) %all-gather.4.cloned.1.call-update) | async-done | bytes 2097168 | tf_op jit(solution)/shard_map/all_gather | solution.py:138
  514.7 4.4 fusion.35
  519.1 1.4 fusion.11
  520.6 1.4 fusion.9
  522.0 1.5 convolution_add_fusion.3
  523.5 1.4 convolution_subtract_fusion.3
  525.1 1.5 fusion.60
  526.6 52.6 %psum.15 = f32[4,2]{0,1:T(2,128)S(1)} all-reduce(f32[4,2]{0,1:T(2,128)S(1)} %pad_maximum_fusion.4), channel_id=1, replica_groups=mesh['tm'=8,'space'=32] {'space'}, use_global_device_ids=true, to_apply=%region_3.4 | all-reduce | flops 8 | bytes 64 | tf_op jit(solution)/shard_map/psum | solution.py:140
  (363 shorter events, 149.7 us)
Async XLA Ops:
  7.2 405.8 %all-reduce.2.cloned.1.call-start = ((), (), s32[]{:S(2)}) async-start(), calls=%async_computation | async-start | bytes 4194304 | tf_op jit(solution)/shard_map/psum | solution.py:120
  178.5 265.2 %copy-start.1 = (s32[4,3]{1,0:T(4,128)S(1)}, s32[4,3]{1,0:T(4,128)}, u32[]{:S(2)}) copy-start(s32[4,3]{1,0:T(4,128)} %param.9) | copy-start | bytes 148
  178.5 265.3 %copy-start = (f32[1,16,2,4096]{3,2,1,0:T(2,128)S(1)}, f32[1,16,2,4096]{3,2,1,0:T(2,128)}, u32[]{:S(2)}) copy-start(f32[1,16,2,4096]{3,2,1,0:T(2,128)} %param.7) | copy-start | bytes 1572868
  178.6 336.1 %all-gather.4.cloned.1.call-start = ((), (), s32[]{:S(2)}) async-start(), calls=%async_computation.1 | async-start | bytes 2162688 | tf_op jit(solution)/shard_map/all_gather | solution.py:138
Sparse Core Ops, SparseCore 0:
  178.7 234.2 all-reduce.1
  443.8 70.8 all-gather.3
where the time goes:
time: 592 us; the launch traced here: 587 us
  waiting for transfers between devices  298 us (50%)
  local copies, waits for them, and re-layouts  90.1 us (15%)
  blocking collectives  81.8 us (14%)
  matrix products  70.7 us (12%)
  other arithmetic  19.1 us (3%)
  between operations  15 us (3%)
  loops' own time  12.2 us (2%)
    psum x1, waiting for transfers between devices, shards(): lax.psum(elemental_rows(vec_re, vec_im, lead_re, lead_im, 0, nvec, factor...  234 us
    all_gather x1, waiting for transfers between devices, shards(): sink_rows = lax.all_gather(sink, 'space', axis=0, tiled=True)  64 us
    dot_general x64, matrix products, contract_first(): lax.dot_general(left, right, (((0,), (0,)), ((), ())), precision=exact_mode)  61.1 us
    psum x1, blocking collectives, shards(): correlator = lax.psum(partial_corr, 'space') * corr_factor  52.6 us
    slice x36, local copies, waits for them, and re-layouts, rotate(): return jnp.concatenate([values[places:], values[:places]], axis=0)  30.9 us
    all_gather x1, blocking collectives, shards(): every_time = lax.all_gather(own[None], 'tm', axis=0, tiled=True)  29.2 us
    another operation x32, local copies, waits for them, and re-layouts, one_block(): stacked = jnp.stack([out_re, out_im], 0).reshape(2, nvec, block, nvec)  17 us
    sub x16, other arithmetic, one_block(): cross_re = (one_re - two_re).reshape(3 * sites, block * nvec)  15.5 us
  transfers between devices with their start and end apart: 2, of which 2 were waited for; matrix products, arithmetic and copies ran while one was open for 1% of the time, Pallas kernels for 0%

commit v1 on v0

v1 whole, which is shorter than its diff:
```python
import functools
import math

import jax
import jax.numpy as jnp
from jax import lax
from jax.experimental import pallas as pl
from jax.experimental.pallas import tpu as pltpu
from jax.sharding import Mesh
from jax.sharding import PartitionSpec as P

F32 = jnp.float32
BF16 = jnp.bfloat16
HALF = 32
STEPS = 16
LEAD = (1, 0, 2)


def split(value):
    high = value.astype(BF16)
    return high, (value - high.astype(F32)).astype(BF16)


def dot_nn(left, right):
    return lax.dot_general(left, right, (((1,), (0,)), ((), ())), preferred_element_type=F32)


def dot_nt(left, right):
    return lax.dot_general(left, right, (((1,), (1,)), ((), ())), preferred_element_type=F32)


def dot_tn(left, right):
    return lax.dot_general(left, right, (((0,), (0,)), ((), ())), preferred_element_type=F32)


def lanes_of(shape):
    return lax.broadcasted_iota(jnp.int32, shape, 1)


def pair_kernel(factor, half_ref, vec_ref, out_ref, ext, lead, cross_high, cross_low):
    half = half_ref[0]
    own = pl.multiple_of(half * HALF, HALF)
    other = pl.multiple_of((1 - half) * HALF, HALF)
    for part in range(2):
        for colour in range(3):
            ext[part * 3 + colour, 0:HALF] = vec_ref[part, colour, pl.ds(own, HALF), :]
            ext[part * 3 + colour, HALF : HALF + STEPS] = vec_ref[part, colour, pl.ds(own, STEPS), :]
    sites = vec_ref.shape[3]
    for colour in range(3):
        at = colour * 2 * sites
        own_re, own_im = ext[colour, 0:HALF], ext[3 + colour, 0:HALF]
        oth_re = vec_ref[0, colour, pl.ds(other, HALF), :]
        oth_im = vec_ref[1, colour, pl.ds(other, HALF), :]
        for place, value in enumerate(
            (
                (own_re, -own_im),
                (own_im, own_re),
                (oth_re, -oth_im),
                (oth_im, oth_re),
            )
        ):
            for side in range(2):
                high, low = split(value[side])
                columns = slice(at + side * sites, at + (side + 1) * sites)
                lead[place * HALF : (place + 1) * HALF, columns] = high
                lead[128 + place * HALF : 128 + (place + 1) * HALF, columns] = low
    for group in range(STEPS // 4):
        rows = slice(group * 128, (group + 1) * 128)
        for inner in range(4):
            step = group * 4 + inner + 1
            here = slice(group * 128 + inner * HALF, group * 128 + (inner + 1) * HALF)
            for colour in range(3):
                one, two = (colour + 1) % 3, (colour + 2) % 3
                one_re, one_im = ext[one, 0:HALF], ext[3 + one, 0:HALF]
                two_re, two_im = ext[two, 0:HALF], ext[3 + two, 0:HALF]
                one_re2, one_im2 = ext[one, step : step + HALF], ext[3 + one, step : step + HALF]
                two_re2, two_im2 = ext[two, step : step + HALF], ext[3 + two, step : step + HALF]
                re = (one_re * two_re2 - one_im * two_im2) - (two_re * one_re2 - two_im * one_im2)
                im = (one_re * two_im2 + one_im * two_re2) - (two_re * one_im2 + two_im * one_re2)
                at = colour * 2 * sites
                for side, value in enumerate((re, im)):
                    high, low = split(value)
                    columns = slice(at + side * sites, at + (side + 1) * sites)
                    cross_high[here, columns] = high
                    cross_low[here, columns] = low
        first = dot_nt(cross_high[rows], lead[...])
        second = dot_nt(cross_low[rows], lead[0:128])
        total = (first[:, 0:128] + first[:, 128:256] + second) * (-factor)
        for inner in range(4):
            out_ref[pl.ds(group * 4 + inner, HALF, stride=STEPS), :] = total[inner * HALF : (inner + 1) * HALF]


def pair_products(half, vec, factor):
    sites = vec.shape[3]
    return pl.pallas_call(
        functools.partial(pair_kernel, factor),
        out_shape=jax.ShapeDtypeStruct((HALF * STEPS, 128), F32),
        in_specs=[pl.BlockSpec(memory_space=pltpu.SMEM), pl.BlockSpec(memory_space=pltpu.VMEM)],
        out_specs=pl.BlockSpec(memory_space=pltpu.VMEM),
        scratch_shapes=[
            pltpu.VMEM((6, HALF + STEPS, sites), F32),
            pltpu.VMEM((256, 6 * sites), BF16),
            pltpu.VMEM((HALF * STEPS, 6 * sites), BF16),
            pltpu.VMEM((HALF * STEPS, 6 * sites), BF16),
        ],
        compiler_params=pltpu.CompilerParams(vmem_limit_bytes=24 << 20),
        name="pair_products",
    )(half, vec)


def swap_parts(value):
    lane = lanes_of(value.shape)
    return jnp.where(lane % 64 < 32, pltpu.roll(value, 96, 1), pltpu.roll(value, 32, 1))


def contract_kernel(place_ref, choice_ref, mine_ref, theirs_ref, sink_ref, peram_ref,
                    rows_ref, corr_ref, pairs, quark, weights, inner):
    core, run = place_ref[0], place_ref[1]
    first = core == 0
    combos = choice_ref.shape[0]

    for s in range(combos):
        for q in range(3):
            spin = choice_ref[s, q]
            parts = []
            for part in range(2):
                top = peram_ref[spin, part, pl.ds(pl.multiple_of(core * HALF, HALF), HALF), :]
                low = peram_ref[spin, part, pl.ds(pl.multiple_of((1 - core) * HALF, HALF), HALF), :]
                both = jnp.concatenate([top, low], axis=0)
                left, right = both[:, 0:HALF], both[:, HALF : 2 * HALF]
                parts.append((jnp.where(first, left, right), jnp.where(first, right, left)))
            (re_own, re_oth), (im_own, im_oth) = parts
            quark[s * 3 + q] = jnp.concatenate([re_own, im_own, re_oth, im_oth], axis=1)

    for s in range(combos):
        for slot in range(3):
            for e in range(2):
                row = s * 6 + slot * 2 + e
                weights[row : row + 1] = quark[s * 3 + LEAD[slot], pl.ds(2 * run + e, 1), :]
    tail = 6 * combos
    shape = (HALF - tail, 128)
    lane, row = lanes_of(shape), lax.broadcasted_iota(jnp.int32, shape, 0)
    number = 4 * run + 2 * core + row
    in_own = (number >= HALF) == (core == 1)
    lit = (number % HALF + jnp.where(in_own, 0, 64)) == lane
    weights[tail:HALF] = jnp.where(lit & (row < 2), 1.0, 0.0)

    for g, from_ref in enumerate((mine_ref, theirs_ref)):
        base = g * HALF * HALF
        pairs[pl.ds(base, HALF, stride=HALF + 1), :] = jnp.zeros((HALF, 128), F32)
        for j in range(HALF):
            straight = min(STEPS, HALF - 1 - j)
            at = base + j * HALF
            if straight:
                pairs[at + j + 1 : at + j + 1 + straight] = from_ref[j * STEPS : j * STEPS + straight]
            if straight < STEPS:
                pairs[at : at + STEPS - straight] = from_ref[j * STEPS + straight : (j + 1) * STEPS]
        for j in range(HALF):
            count = STEPS - 1
            straight = min(count, HALF - 1 - j)
            if straight:
                pairs[pl.ds(base + (j + 1) * HALF + j, straight, stride=HALF), :] = -from_ref[j * STEPS : j * STEPS + straight]
            if straight < count:
                pairs[pl.ds(base + j, count - straight, stride=HALF), :] = -from_ref[j * STEPS + straight : j * STEPS + count]

    lead = weights[...]
    wide = lanes_of((HALF, 128))
    sign = jnp.where(wide % 64 < 32, 1.0, -1.0)
    lead_high, lead_low = split(lead)
    conj_high, conj_low = split(lead * sign)
    blank = jnp.zeros((HALF, 64), BF16)
    for g in range(2):
        here = slice(g * 64, g * 64 + 64)
        there = slice(64 - g * 64, 128 - g * 64)
        left_r = jnp.concatenate(
            [
                jnp.concatenate([-lead_high[:, here], -lead_high[:, here]], axis=1),
                jnp.concatenate([-lead_low[:, here], blank], axis=1),
            ],
            axis=0,
        )
        left_n = jnp.concatenate(
            [
                jnp.concatenate([conj_high[:, there], conj_high[:, there]], axis=1),
                jnp.concatenate([conj_low[:, there], blank], axis=1),
            ],
            axis=0,
        )
        for b in range(0, HALF, 2):
            right_r, right_n = [], []
            for e in range(2):
                at = (g * HALF + b + e) * HALF
                value = pairs[at : at + HALF]
                turned = -swap_parts(value) * sign
                parts, packs = [], []
                for one in (value, turned):
                    high = one.astype(BF16)
                    low = one - high.astype(F32)
                    parts.append((high, low.astype(BF16)))
                    packs.append(jnp.where(wide < 64, pltpu.roll(high.astype(F32), 64, 1), low))
                right_r.append(jnp.concatenate([parts[0][0], parts[1][0], parts[0][1], parts[1][1]], axis=0))
                right_n += [packs[0].astype(BF16), (-packs[1]).astype(BF16)]
            some = dot_nn(left_r, jnp.concatenate(right_r, axis=1))
            some = some[0:HALF] + some[HALF : 2 * HALF]
            more = dot_nt(left_n, jnp.concatenate(right_n, axis=0))
            more = more[0:HALF] + more[HALF : 2 * HALF]
            for e in range(2):
                extra = more if e == 0 else pltpu.roll(more, 64, 1)
                result = some[:, e * 128 : (e + 1) * 128] + jnp.where(wide < 64, extra, 0.0)
                if g == 1:
                    result = pltpu.roll(result, 64, 1)
                inner[pl.ds(g * HALF + b + e, HALF, stride=64), :] = result

    for e in range(2):
        at = (tail + e) * 64
        value = inner[at : at + 64]
        shape = (64, 64)
        mixed = (lax.broadcasted_iota(jnp.int32, shape, 0) < HALF) != (lanes_of(shape) < HALF)
        for part in range(2):
            one = jnp.concatenate(
                [value[:, part * 32 : part * 32 + 32], value[:, 64 + part * 32 : 96 + part * 32]], axis=1
            )
            one = one - jnp.where(mixed, one, 0.0).T
            top = jnp.where(first, one[0:HALF], one[HALF:64])
            low = jnp.where(first, one[HALF:64], one[0:HALF])
            both = jnp.concatenate([top, low], axis=0)
            left, right = both[:, 0:HALF], both[:, HALF:64]
            rows_ref[e, part] = jnp.concatenate(
                [jnp.where(first, left, right), jnp.where(first, right, left)], axis=1
            )

    shape = (STEPS, 128)
    step = lax.broadcasted_iota(jnp.int32, shape, 0)
    share = jnp.where(lanes_of(shape) < 64, 1.0 / 3.0, 1.0) * jnp.where(step == STEPS - 1, 0.5, 1.0)
    sink = []
    for e in range(2):
        shape = (HALF, STEPS)
        target = (2 * run + e + lanes_of(shape) + 1) % HALF
        move = jnp.where(lax.broadcasted_iota(jnp.int32, shape, 0) == target, 1.0, 0.0).astype(BF16)
        high, low = split(sink_ref[e * STEPS : (e + 1) * STEPS] * share)
        placed = dot_nn(move, high) + dot_nn(move, low)
        for part in range(2):
            one = jnp.concatenate(
                [placed[:, part * 32 : part * 32 + 32], placed[:, 64 + part * 32 : 96 + part * 32]], axis=1
            )
            one = jnp.concatenate([one, jnp.zeros((HALF, 64), F32)], axis=0)
            sink.append(one - one.T)
    sink_high, sink_low = split(jnp.concatenate(sink, axis=1))
    sink_stack = jnp.concatenate([sink_high, sink_low, sink_high], axis=0)

    shape = (128, 128)
    row, lane = lax.broadcasted_iota(jnp.int32, shape, 0), lanes_of(shape)
    cross = (row % 64 < HALF) != (lane < 64)
    side = jnp.where(lanes_of((64, 128)) < 64, 1.0, -1.0)
    plain = jnp.where(lanes_of((64, 128)) % 64 < 32, 1.0, -1.0)
    results = []
    for s in range(combos):
        dual, both = [], []
        for q in range(3):
            value = quark[s * 3 + q]
            high, low = split(value)
            out = dot_tn(jnp.concatenate([high, high, low], axis=0), sink_stack)
            re = jnp.concatenate([out[0:32], out[64:96]], axis=0)
            im = jnp.concatenate([out[32:64], out[96:128]], axis=0)
            per_row = []
            for e in range(2):
                re_e, im_e = re[:, e * 128 : (e + 1) * 128], im[:, e * 128 : (e + 1) * 128]
                per_row.append(
                    (
                        re_e + pltpu.roll(im_e, 64, 1) * side,
                        im_e - pltpu.roll(re_e, 64, 1) * side,
                    )
                )
            dual.append(per_row)
            full_high, full_low = split(jnp.concatenate([value * plain, swap_parts(value)], axis=0))
            both.append(jnp.concatenate([full_high, full_low], axis=0))
        at = s * 6 * 64
        blocks = [inner[at + slot * 128 : at + (slot + 1) * 128] for slot in range(3)]
        masked = [jnp.where(cross, block, 0.0) for block in blocks]
        acc_re, acc_im = jnp.zeros((64, 128), F32), jnp.zeros((64, 128), F32)
        for q, lefts, partners in (
            (2, (blocks[0], blocks[1]), (0, 1)),
            (1, (blocks[2], masked[1]), (0, 2)),
            (0, (masked[0], masked[2]), (2, 1)),
        ):
            high, low = split(jnp.concatenate(lefts, axis=0))
            out = dot_nt(high, both[q])
            out = out[:, 0:128] + out[:, 128:256] + dot_nt(low, both[q][0:128])
            for k in range(2):
                for e in range(2):
                    part = out[(k * 2 + e) * 64 : (k * 2 + e + 1) * 64]
                    acc_re += part * dual[partners[k]][e][0]
                    acc_im += part * dual[partners[k]][e][1]
        results += [jnp.sum(acc_re, axis=0, keepdims=True), jnp.sum(acc_im, axis=0, keepdims=True)]
    table = jnp.sum(jnp.concatenate(results, axis=0), axis=1, keepdims=True)
    shape = (2 * combos, 128)
    spread = jnp.where(lax.broadcasted_iota(jnp.int32, shape, 0) == lanes_of(shape), table, 0.0)
    corr_ref[...] = jnp.broadcast_to(jnp.sum(spread, axis=0, keepdims=True), corr_ref.shape)


def contract(place, choice, mine, theirs, sink, peram, copies):
    smem = pl.BlockSpec(memory_space=pltpu.SMEM)
    vmem = pl.BlockSpec(memory_space=pltpu.VMEM)
    return pl.pallas_call(
        contract_kernel,
        out_shape=(
            jax.ShapeDtypeStruct((2, 2, 64, 64), F32),
            jax.ShapeDtypeStruct((copies, 128), F32),
        ),
        in_specs=[smem, smem, vmem, vmem, vmem, vmem],
        out_specs=(vmem, vmem),
        scratch_shapes=[
            pltpu.VMEM((2 * HALF * HALF, 128), F32),
            pltpu.VMEM((12, 64, 128), F32),
            pltpu.VMEM((HALF, 128), F32),
            pltpu.VMEM((HALF * 64, 128), F32),
        ],
        compiler_params=pltpu.CompilerParams(vmem_limit_bytes=24 << 20),
        name="contract",
    )(place, choice, mine, theirs, sink, peram)


def swapped(value, axis, mask):
    count = lax.axis_size(axis)
    return lax.ppermute(value, axis, [(i, i ^ mask) for i in range(count)])


def shards(vectors, perambulators, shift_steps, spin_choice):
    vec = vectors[0]
    nvec = vec.shape[2]
    z_count, run_count = lax.axis_size("z"), lax.axis_size("z") * lax.axis_size("yl")
    space_count = run_count * lax.axis_size("core")
    combos = spin_choice.shape[0]
    factor = 1.0 / math.sqrt(24.0 * vec.shape[3] * space_count)
    corr_factor = 0.25 / (nvec * math.sqrt(nvec))
    core = lax.axis_index("core")
    run = lax.axis_index("z") * lax.axis_size("yl") + lax.axis_index("yl")
    peram = perambulators[0].reshape(-1, 2, nvec, nvec)

    away = pair_products((1 - core)[None], vec, factor)
    got = swapped(away, "core", 1)
    keep = pair_products(core[None], vec, factor)
    part = (keep + got).reshape(run_count, -1, 128)
    own = lax.all_to_all(part, ("z", "yl"), 0, 0, tiled=True).sum(0)

    near = jnp.stack([own, swapped(own, "yh", 1)])
    every = jnp.broadcast_to(own[None], (run_count,) + own.shape)
    mine = lax.all_to_all(every, ("z", "yl"), 0, 0, tiled=True).reshape(-1, 128)
    theirs = swapped(mine, "core", 1)
    wider = jnp.concatenate([near, swapped(near, "x", 1)])
    all_times = jnp.concatenate([wider, swapped(wider, "x", 2)])
    now = lax.axis_index("yh") * lax.axis_size("x") + lax.axis_index("x")
    away_by = now ^ ((now + shift_steps[0]) % 8)
    pick = (away_by & 2) * 2 + (away_by & 1) * 2 + (away_by >> 2)
    sink = lax.dynamic_index_in_dim(all_times, pick, 0, keepdims=False)

    place = jnp.stack([core, run]).astype(jnp.int32)
    rows, corr = contract(place, spin_choice, mine, theirs, sink, peram, space_count)
    total = lax.all_to_all(corr, ("z", "yl", "core"), 0, 0, tiled=True).sum(0)
    correlator = total[: 2 * combos].reshape(1, combos, 2) * corr_factor
    return (rows.reshape(1, 2, 2, nvec * nvec)[0], correlator)


def solution(mesh):
    fine = Mesh(mesh.devices.reshape(2, 4, 8, 2, 2), ("yh", "x", "z", "yl", "core"))
    times, space = ("yh", "x"), ("z", "yl", "core")
    placed = (P(times, None, None, None, space), P(times, None, None, None), P(times), P())

    def whole(vectors, perambulators, shift_steps, spin_choice):
        rows, correlator = shards(vectors, perambulators, shift_steps, spin_choice)
        return rows[None], correlator

    return jax.shard_map(
        whole,
        mesh=fine,
        in_specs=placed,
        out_specs=(P(times, space, None, None), P(times, None, None)),
        check_vma=False,
    )
```

time: 592 us -> 84.1 us (0.14)
  waiting for transfers between devices: 298 us -> 14 us
  local copies, waits for them, and re-layouts: 90.1 us -> 3.82 us
  matrix products: 70.7 us -> 0 us
  blocking collectives: 81.8 us -> 18.8 us
  starting transfers between devices: 0.08 us -> 23.3 us
  Pallas kernels: 0 us -> 22.2 us
  other arithmetic: 19.1 us -> 0.2 us
  between operations: 15 us -> 1.42 us
  loops' own time: 12.2 us -> 0 us
    psum x1 -> x0, waiting for transfers between devices: 234 us -> none  [shards(): lax.psum(elemental_rows(vec_re, vec_im, lead_re, lead_im, 0, nvec, factor...]
    dot_general x77 -> x0, matrix products: 70.7 us -> none  [the longest x64 61.1 us: contract_first(): lax.dot_general(left, right, (((0,), (0,)), ((), ())), precision=exact_mode)]
    all_gather x1 -> x0, waiting for transfers between devices: 64 us -> none  [shards(): sink_rows = lax.all_gather(sink, 'space', axis=0, tiled=True)]
    psum x1 -> x0, blocking collectives: 52.6 us -> none  [shards(): correlator = lax.psum(partial_corr, 'space') * corr_factor]
    slice x40 -> x0, local copies, waits for them, and re-layouts: 37.5 us -> none  [the longest x36 30.9 us: rotate(): return jnp.concatenate([values[places:], values[:places]], axis=0)]
    all_gather x1 -> x0, blocking collectives: 29.2 us -> none  [shards(): every_time = lax.all_gather(own[None], 'tm', axis=0, tiled=True)]
    pallas_call x0 -> x3, Pallas kernels: none -> 22.2 us  [the longest x1 18 us: contract(): pl.pallas_call(contract_kernel, out_shape=(jax.ShapeDtypeStruct((2, 2, 64...]
    all_to_all x0 -> x1, blocking collectives: none -> 18.8 us  [shards(): own = lax.all_to_all(part, ('z', 'yl'), 0, 0, tiled=True).sum(0)]
  transfers between devices with their start and end apart: 2 -> 7, of which waited for: 2 -> 4; matrix products, arithmetic and copies ran while one was open for 1% -> 2% of each run, Pallas kernels for 0% -> 3%
where the time goes in v1:
time: 84.1 us; the launch traced here: 83.8 us
  starting transfers between devices  23.3 us (28%)
  Pallas kernels  22.2 us (26%)
  blocking collectives  18.8 us (22%)
  waiting for transfers between devices  14 us (17%)
  local copies, waits for them, and re-layouts  3.82 us (5%)
  between operations  1.42 us (2%)
    all_to_all x1, blocking collectives, shards(): own = lax.all_to_all(part, ('z', 'yl'), 0, 0, tiled=True).sum(0)  18.8 us
    pallas_call x1, Pallas kernels, contract(): pl.pallas_call(contract_kernel, out_shape=(jax.ShapeDtypeStruct((2, 2, 64...  18 us
    ppermute x5, starting transfers between devices, swapped(): return lax.ppermute(value, axis, [(i, i ^ mask) for i in range(count)])  13.6 us
    all_to_all x1, waiting for transfers between devices, shards(): total = lax.all_to_all(corr, ('z', 'yl', 'core'), 0, 0, tiled=True).sum(0)  7.08 us
    all_to_all x1, starting transfers between devices, shards(): total = lax.all_to_all(corr, ('z', 'yl', 'core'), 0, 0, tiled=True).sum(0)  6.24 us
    pallas_call x2, Pallas kernels, pair_products(): pl.pallas_call(functools.partial(pair_kernel, factor), out_shape=jax.Shap...  4.2 us
    ppermute x5, waiting for transfers between devices, swapped(): return lax.ppermute(value, axis, [(i, i ^ mask) for i in range(count)])  3.9 us
    all_to_all x1, starting transfers between devices, shards(): mine = lax.all_to_all(every, ('z', 'yl'), 0, 0, tiled=True).reshape(-1, 128)  3.53 us
  transfers between devices with their start and end apart: 7, of which 4 were waited for; matrix products, arithmetic and copies ran while one was open for 2% of the time, Pallas kernels for 3%

profile of v1, /device:TPU:1, one launch (start us, length us, event | category | flops | bytes accessed | tf_op | source)
XLA Modules:
  0.0 83.8 jit_solution(12153493733433093397)
XLA Ops:
  0.6 1.0 %copy-done = f32[1,2,3,64,256]{4,3,2,1,0:T(8,128)S(1)} copy-done((f32[1,2,3,64,256]{4,3,2,1,0:T(8,128)S(1)}, f32[1,2,3,64,256]{4,3,2,1,0:T(8,128)}, u32[]{:S(2)}) %copy-start) | copy-done | bytes 393240
  1.6 2.1 %pair_products.3 = f32[512,128]{1,0:T(8,128)S(1)} custom-call(s32[1]{0:T(128)} %bitcast.3.half_ref, f32[2,3,64,256]{3,2,1,0:T(8,128)S(1)} %bitcast.17), custom_call_target="tpu_custom_call" | custom-call | tf_op jit(solution)/shard_map/pair_products/pallas_call | solution.py:95
  3.7 3.3 %collective-permute-start = (f32[512,128]{1,0:T(8,128)S(1)}, f32[512,128]{1,0:T(8,128)S(1)}, u32[]{:S(2)}, u32[]{:S(2)}) collective-permute-start(f32[512,128]{1,0:T(8,128)S(1)} %pair_products.3), channel_id=1, source_target_pairs={{0,1},{1,0},{2,3},{3,2},{4,5},{5,4},{6,7},{7,6},{8,9},{9,8},{10,11... | collective-permute-start | bytes 786440 | tf_op jit(solution)/shard_map/ppermute | solution.py:325
  7.1 2.1 %pair_products.2 = f32[512,128]{1,0:T(8,128)S(1)} custom-call(s32[1]{0:T(128)} %bitcast.half_ref, f32[2,3,64,256]{3,2,1,0:T(8,128)S(1)} %bitcast.18), custom_call_target="tpu_custom_call" | custom-call | tf_op jit(solution)/shard_map/pair_products/pallas_call | solution.py:95
  9.2 18.8 %all_to_all.19 = f32[16,32,128]{2,1,0:T(8,128)S(1)} all-to-all(f32[16,32,128]{2,1,0:T(8,128)S(1)} %bitcast.21), channel_id=1, replica_groups=mesh['yh'=2,'x'=4,'z'=8,'yl'=2,'core'=2] {'z','yl'}, dimensions={0} | all-to-all | bytes 524288 | tf_op jit(solution)/shard_map/all_to_all | solution.py:344
  28.1 0.0 copy-start.3
  28.1 0.7 broadcast_in_dim.13
  28.8 3.5 %all-to-all-start.1 = ((f32[16,32,128]{2,1,0:T(8,128)}), f32[16,32,128]{2,1,0:T(8,128)S(1)}, u32[]{:S(2)}, u32[]{:S(2)}) async-start(f32[16,32,128]{2,1,0:T(8,128)} %broadcast_in_dim.13), calls=%async_computation.1 | async-start | bytes 524288 | tf_op jit(solution)/shard_map/all_to_all | solution.py:348
  32.3 2.7 %collective-permute-start.2 = (f32[32,128]{1,0:T(8,128)S(1)}, f32[32,128]{1,0:T(8,128)S(1)}, u32[]{:S(2)}, u32[]{:S(2)}) collective-permute-start(f32[32,128]{1,0:T(8,128)S(1)} %reduce_sum.18), channel_id=1, source_target_pairs={{0,128},{128,0},{1,129},{129,1},{2,130},{130,2},{3,131},{131,3},{4... | collective-permute-start | bytes 49160 | tf_op jit(solution)/shard_map/ppermute | solution.py:325
  35.0 1.5 %collective-permute-done.2 = f32[32,128]{1,0:T(8,128)S(1)} collective-permute-done((f32[32,128]{1,0:T(8,128)S(1)}, f32[32,128]{1,0:T(8,128)S(1)}, u32[]{:S(2)}, u32[]{:S(2)}) %collective-permute-start.2) | collective-permute-done | bytes 16416 | tf_op jit(solution)/shard_map/ppermute | solution.py:325
  36.5 1.2 %collective-permute-start.3 = (f32[2,32,128]{2,1,0:T(8,128)S(1)}, f32[2,32,128]{2,1,0:T(8,128)S(1)}, u32[]{:S(2)}, u32[]{:S(2)}) collective-permute-start(f32[2,32,128]{2,1,0:T(8,128)S(1)} %pad_maximum_fusion.1), channel_id=1, source_target_pairs={{0,32},{32,0},{64,96},{96,64},{1,33},{33,1},{65,97},{97,65},{2,34}... | collective-permute-start | bytes 98312 | tf_op jit(solution)/shard_map/ppermute | solution.py:325
  38.4 0.6 reshape_squeeze.3.peram_ref
  39.0 3.0 %all-to-all-done.1 = f32[16,32,128]{2,1,0:T(8,128)S(1)} async-done(((f32[16,32,128]{2,1,0:T(8,128)}), f32[16,32,128]{2,1,0:T(8,128)S(1)}, u32[]{:S(2)}, u32[]{:S(2)}) %all-to-all-start.1) | async-done | bytes 262176 | tf_op jit(solution)/shard_map/all_to_all | solution.py:348
  42.0 3.3 %collective-permute-start.1 = (f32[512,128]{1,0:T(8,128)S(1)}, f32[512,128]{1,0:T(8,128)S(1)}, u32[]{:S(2)}, u32[]{:S(2)}) collective-permute-start(f32[512,128]{1,0:T(8,128)S(1)} %bitcast.19), channel_id=1, source_target_pairs={{0,1},{1,0},{2,3},{3,2},{4,5},{5,4},{6,7},{7,6},{8,9},{9,8},{10,11... | collective-permute-start | bytes 786440 | tf_op jit(solution)/shard_map/ppermute | solution.py:325
  45.4 3.0 %collective-permute-start.4 = (f32[4,32,128]{2,1,0:T(8,128)S(1)}, f32[4,32,128]{2,1,0:T(8,128)S(1)}, u32[]{:S(2)}, u32[]{:S(2)}) collective-permute-start(f32[4,32,128]{2,1,0:T(8,128)S(1)} %pad_maximum_fusion), channel_id=1, source_target_pairs={{0,64},{32,96},{64,0},{96,32},{1,65},{33,97},{65,1},{97,33},{2,66}... | collective-permute-start | bytes 196616 | tf_op jit(solution)/shard_map/ppermute | solution.py:325
  48.4 0.1 pad_add_fusion.place_ref
  48.5 2.4 %collective-permute-done.4 = f32[4,32,128]{2,1,0:T(8,128)S(1)} collective-permute-done((f32[4,32,128]{2,1,0:T(8,128)S(1)}, f32[4,32,128]{2,1,0:T(8,128)S(1)}, u32[]{:S(2)}, u32[]{:S(2)}) %collective-permute-start.4) | collective-permute-done | bytes 65568 | tf_op jit(solution)/shard_map/ppermute | solution.py:325
  50.9 18.0 %contract.1 = (f32[2,2,64,64]{3,2,1,0:T(8,128)S(1)}, f32[32,128]{1,0:T(8,128)}) custom-call(s32[2]{0:T(128)S(1)} %pad_add_fusion.place_ref, s32[4,3]{1,0:T(4,128)S(1)} %copy-done.2, f32[512,128]{1,0:T(8,128)S(1)} %bitcast.20, f32[512,128]{1,0:T(8,128)S(1)} %collective-permute-done.1.theirs_ref, f32[32,128]{1,0:T(8,128)S(1)} %fusion.3.sink_ref, ...), custom_call_target="tpu_custom_call" | custom-call | tf_op jit(solution)/shard_map/contract/pallas_call | solution.py:304
  68.9 6.2 %all-to-all-start.2 = ((f32[32,1,128]{2,1,0:T(1,128)}), f32[32,1,128]{2,1,0:T(1,128)S(1)}, u32[]{:S(2)}, u32[]{:S(2)}) async-start(f32[32,1,128]{2,1,0:T(1,128)} %bitcast.11), calls=%async_computation.2 | async-start | bytes 32768 | tf_op jit(solution)/shard_map/all_to_all | solution.py:359
  75.1 0.7 broadcast_in_dim_squeeze_reshape.3
  75.9 7.1 %all-to-all-done.2 = f32[32,1,128]{2,1,0:T(1,128)S(1)} async-done(((f32[32,1,128]{2,1,0:T(1,128)}), f32[32,1,128]{2,1,0:T(1,128)S(1)}, u32[]{:S(2)}, u32[]{:S(2)}) %all-to-all-start.2) | async-done | bytes 16416 | tf_op jit(solution)/shard_map/all_to_all | solution.py:359
  83.0 0.1 reduce_sum.19
  83.0 0.1 mul.28
  83.1 0.7 copy.9
  (15 shorter events, 0.1 us)
Async XLA Ops:
  0.6 1.0 %copy-start = (f32[1,2,3,64,256]{4,3,2,1,0:T(8,128)S(1)}, f32[1,2,3,64,256]{4,3,2,1,0:T(8,128)}, u32[]{:S(2)}) copy-start(f32[1,2,3,64,256]{4,3,2,1,0:T(8,128)} %param.4) | copy-start | bytes 1179652
  1.6 5.4 %copy-start.1 = (f32[1,2,3,64,256]{4,3,2,1,0:T(8,128)S(1)}, f32[1,2,3,64,256]{4,3,2,1,0:T(8,128)}, u32[]{:S(2)}) copy-start(f32[1,2,3,64,256]{4,3,2,1,0:T(8,128)} %param.4) | copy-start | bytes 1179652
  3.7 5.4 %collective-permute-start = (f32[512,128]{1,0:T(8,128)S(1)}, f32[512,128]{1,0:T(8,128)S(1)}, u32[]{:S(2)}, u32[]{:S(2)}) collective-permute-start(f32[512,128]{1,0:T(8,128)S(1)} %pair_products.3), channel_id=1, source_target_pairs={{0,1},{1,0},{2,3},{3,2},{4,5},{5,4},{6,7},{7,6},{8,9},{9,8},{10,11... | collective-permute-start | bytes 786440 | tf_op jit(solution)/shard_map/ppermute | solution.py:325
  28.1 10.3 %copy-start.3 = (f32[1,16,2,4096]{3,2,1,0:T(2,128)S(1)}, f32[1,16,2,4096]{3,2,1,0:T(2,128)}, u32[]{:S(2)}) copy-start(f32[1,16,2,4096]{3,2,1,0:T(2,128)} %param.5) | copy-start | bytes 1572868
  28.8 13.3 %all-to-all-start.1 = ((f32[16,32,128]{2,1,0:T(8,128)}), f32[16,32,128]{2,1,0:T(8,128)S(1)}, u32[]{:S(2)}, u32[]{:S(2)}) async-start(f32[16,32,128]{2,1,0:T(8,128)} %broadcast_in_dim.13), calls=%async_computation.1 | async-start | bytes 524288 | tf_op jit(solution)/shard_map/all_to_all | solution.py:348
  32.3 4.2 %collective-permute-start.2 = (f32[32,128]{1,0:T(8,128)S(1)}, f32[32,128]{1,0:T(8,128)S(1)}, u32[]{:S(2)}, u32[]{:S(2)}) collective-permute-start(f32[32,128]{1,0:T(8,128)S(1)} %reduce_sum.18), channel_id=1, source_target_pairs={{0,128},{128,0},{1,129},{129,1},{2,130},{130,2},{3,131},{131,3},{4... | collective-permute-start | bytes 49160 | tf_op jit(solution)/shard_map/ppermute | solution.py:325
  36.5 8.9 %collective-permute-start.3 = (f32[2,32,128]{2,1,0:T(8,128)S(1)}, f32[2,32,128]{2,1,0:T(8,128)S(1)}, u32[]{:S(2)}, u32[]{:S(2)}) collective-permute-start(f32[2,32,128]{2,1,0:T(8,128)S(1)} %pad_maximum_fusion.1), channel_id=1, source_target_pairs={{0,32},{32,0},{64,96},{96,64},{1,33},{33,1},{65,97},{97,65},{2,34}... | collective-permute-start | bytes 98312 | tf_op jit(solution)/shard_map/ppermute | solution.py:325
  42.0 8.9 %collective-permute-start.1 = (f32[512,128]{1,0:T(8,128)S(1)}, f32[512,128]{1,0:T(8,128)S(1)}, u32[]{:S(2)}, u32[]{:S(2)}) collective-permute-start(f32[512,128]{1,0:T(8,128)S(1)} %bitcast.19), channel_id=1, source_target_pairs={{0,1},{1,0},{2,3},{3,2},{4,5},{5,4},{6,7},{7,6},{8,9},{9,8},{10,11... | collective-permute-start | bytes 786440 | tf_op jit(solution)/shard_map/ppermute | solution.py:325
  45.4 5.5 %collective-permute-start.4 = (f32[4,32,128]{2,1,0:T(8,128)S(1)}, f32[4,32,128]{2,1,0:T(8,128)S(1)}, u32[]{:S(2)}, u32[]{:S(2)}) collective-permute-start(f32[4,32,128]{2,1,0:T(8,128)S(1)} %pad_maximum_fusion), channel_id=1, source_target_pairs={{0,64},{32,96},{64,0},{96,32},{1,65},{33,97},{65,1},{97,33},{2,66}... | collective-permute-start | bytes 196616 | tf_op jit(solution)/shard_map/ppermute | solution.py:325
  48.5 2.4 %copy-start.2 = (s32[4,3]{1,0:T(4,128)S(1)}, s32[4,3]{1,0:T(4,128)}, u32[]{:S(2)}) copy-start(s32[4,3]{1,0:T(4,128)} %choice_ref.1) | copy-start | bytes 148
  68.9 14.1 %all-to-all-start.2 = ((f32[32,1,128]{2,1,0:T(1,128)}), f32[32,1,128]{2,1,0:T(1,128)S(1)}, u32[]{:S(2)}, u32[]{:S(2)}) async-start(f32[32,1,128]{2,1,0:T(1,128)} %bitcast.11), calls=%async_computation.2 | async-start | bytes 32768 | tf_op jit(solution)/shard_map/all_to_all | solution.py:359

commit v2 on v1

--- a/solution.py
+++ b/solution.py
@@ -113,12 +113,19 @@
     return jnp.where(lane % 64 < 32, pltpu.roll(value, 96, 1), pltpu.roll(value, 32, 1))
 
 
-def contract_kernel(place_ref, choice_ref, mine_ref, theirs_ref, sink_ref, peram_ref,
-                    rows_ref, corr_ref, pairs, quark, weights, inner):
+def turned(value, sign):
+    return -swap_parts(value) * sign
+
+
+def part_signs(shape):
+    return jnp.where(lanes_of(shape) % 64 < 32, 1.0, -1.0)
+
+
+def prepare_kernel(place_ref, choice_ref, peram_ref, left_r_ref, left_n_ref, flipped_ref, full_ref, quark, weights):
     core, run = place_ref[0], place_ref[1]
     first = core == 0
     combos = choice_ref.shape[0]
-
+    plain = part_signs((64, 128))
     for s in range(combos):
         for q in range(3):
             spin = choice_ref[s, q]
@@ -130,7 +137,12 @@
                 left, right = both[:, 0:HALF], both[:, HALF : 2 * HALF]
                 parts.append((jnp.where(first, left, right), jnp.where(first, right, left)))
             (re_own, re_oth), (im_own, im_oth) = parts
-            quark[s * 3 + q] = jnp.concatenate([re_own, im_own, re_oth, im_oth], axis=1)
+            value = jnp.concatenate([re_own, im_own, re_oth, im_oth], axis=1)
+            quark[s * 3 + q] = value
+            high, low = split(value.T)
+            flipped_ref[s * 3 + q] = jnp.concatenate([high, high, low], axis=1)
+            full_high, full_low = split(jnp.concatenate([value * plain, swap_parts(value)], axis=0))
+            full_ref[s * 3 + q] = jnp.concatenate([full_high, full_low], axis=0)
 
     for s in range(combos):
         for slot in range(3):
@@ -145,6 +157,21 @@
     lit = (number % HALF + jnp.where(in_own, 0, 64)) == lane
     weights[tail:HALF] = jnp.where(lit & (row < 2), 1.0, 0.0)
 
+    lead = weights[...]
+    sign = part_signs((HALF, 128))
+    lead_high, lead_low = split(lead)
+    conj_high, conj_low = split(lead * sign)
+    blank = jnp.zeros((HALF, 64), BF16)
+    for g in range(2):
+        here = slice(g * 64, g * 64 + 64)
+        there = slice(64 - g * 64, 128 - g * 64)
+        left_r_ref[g, 0:HALF] = jnp.concatenate([-lead_high[:, here], -lead_high[:, here]], axis=1)
+        left_r_ref[g, HALF : 2 * HALF] = jnp.concatenate([-lead_low[:, here], blank], axis=1)
+        left_n_ref[g, 0:HALF] = jnp.concatenate([conj_high[:, there], conj_high[:, there]], axis=1)
+        left_n_ref[g, HALF : 2 * HALF] = jnp.concatenate([conj_low[:, there], blank], axis=1)
+
+
+def first_index_kernel(left_r_ref, left_n_ref, mine_ref, theirs_ref, inner, pairs):
     for g, from_ref in enumerate((mine_ref, theirs_ref)):
         base = g * HALF * HALF
         pairs[pl.ds(base, HALF, stride=HALF + 1), :] = jnp.zeros((HALF, 128), F32)
@@ -163,37 +190,17 @@
             if straight < count:
                 pairs[pl.ds(base + j, count - straight, stride=HALF), :] = -from_ref[j * STEPS + straight : j * STEPS + count]
 
-    lead = weights[...]
     wide = lanes_of((HALF, 128))
-    sign = jnp.where(wide % 64 < 32, 1.0, -1.0)
-    lead_high, lead_low = split(lead)
-    conj_high, conj_low = split(lead * sign)
-    blank = jnp.zeros((HALF, 64), BF16)
+    sign = part_signs((HALF, 128))
     for g in range(2):
-        here = slice(g * 64, g * 64 + 64)
-        there = slice(64 - g * 64, 128 - g * 64)
-        left_r = jnp.concatenate(
-            [
-                jnp.concatenate([-lead_high[:, here], -lead_high[:, here]], axis=1),
-                jnp.concatenate([-lead_low[:, here], blank], axis=1),
-            ],
-            axis=0,
-        )
-        left_n = jnp.concatenate(
-            [
-                jnp.concatenate([conj_high[:, there], conj_high[:, there]], axis=1),
-                jnp.concatenate([conj_low[:, there], blank], axis=1),
-            ],
-            axis=0,
-        )
+        left_r, left_n = left_r_ref[g], left_n_ref[g]
         for b in range(0, HALF, 2):
             right_r, right_n = [], []
             for e in range(2):
                 at = (g * HALF + b + e) * HALF
                 value = pairs[at : at + HALF]
-                turned = -swap_parts(value) * sign
                 parts, packs = [], []
-                for one in (value, turned):
+                for one in (value, turned(value, sign)):
                     high = one.astype(BF16)
                     low = one - high.astype(F32)
                     parts.append((high, low.astype(BF16)))
@@ -211,9 +218,12 @@
                     result = pltpu.roll(result, 64, 1)
                 inner[pl.ds(g * HALF + b + e, HALF, stride=64), :] = result
 
+
+def rows_kernel(place_ref, inner_ref, rows_ref):
+    first = place_ref[0] == 0
+    tail = HALF - 8
     for e in range(2):
-        at = (tail + e) * 64
-        value = inner[at : at + 64]
+        value = inner_ref[(tail + e) * 64 : (tail + e + 1) * 64]
         shape = (64, 64)
         mixed = (lax.broadcasted_iota(jnp.int32, shape, 0) < HALF) != (lanes_of(shape) < HALF)
         for part in range(2):
@@ -229,6 +239,10 @@
                 [jnp.where(first, left, right), jnp.where(first, right, left)], axis=1
             )
 
+
+def correlate_kernel(place_ref, sink_ref, flipped_ref, full_ref, inner_ref, corr_ref):
+    run = place_ref[1]
+    combos = flipped_ref.shape[0] // 3
     shape = (STEPS, 128)
     step = lax.broadcasted_iota(jnp.int32, shape, 0)
     share = jnp.where(lanes_of(shape) < 64, 1.0 / 3.0, 1.0) * jnp.where(step == STEPS - 1, 0.5, 1.0)
@@ -252,14 +266,11 @@
     row, lane = lax.broadcasted_iota(jnp.int32, shape, 0), lanes_of(shape)
     cross = (row % 64 < HALF) != (lane < 64)
     side = jnp.where(lanes_of((64, 128)) < 64, 1.0, -1.0)
-    plain = jnp.where(lanes_of((64, 128)) % 64 < 32, 1.0, -1.0)
     results = []
     for s in range(combos):
-        dual, both = [], []
+        dual = []
         for q in range(3):
-            value = quark[s * 3 + q]
-            high, low = split(value)
-            out = dot_tn(jnp.concatenate([high, high, low], axis=0), sink_stack)
+            out = dot_nn(flipped_ref[s * 3 + q], sink_stack)
             re = jnp.concatenate([out[0:32], out[64:96]], axis=0)
             im = jnp.concatenate([out[32:64], out[96:128]], axis=0)
             per_row = []
@@ -272,10 +283,8 @@
                     )
                 )
             dual.append(per_row)
-            full_high, full_low = split(jnp.concatenate([value * plain, swap_parts(value)], axis=0))
-            both.append(jnp.concatenate([full_high, full_low], axis=0))
         at = s * 6 * 64
-        blocks = [inner[at + slot * 128 : at + (slot + 1) * 128] for slot in range(3)]
+        blocks = [inner_ref[at + slot * 128 : at + (slot + 1) * 128] for slot in range(3)]
         masked = [jnp.where(cross, block, 0.0) for block in blocks]
         acc_re, acc_im = jnp.zeros((64, 128), F32), jnp.zeros((64, 128), F32)
         for q, lefts, partners in (
@@ -284,8 +293,8 @@
             (0, (masked[0], masked[2]), (2, 1)),
         ):
             high, low = split(jnp.concatenate(lefts, axis=0))
-            out = dot_nt(high, both[q])
-            out = out[:, 0:128] + out[:, 128:256] + dot_nt(low, both[q][0:128])
+            out = dot_nt(high, full_ref[s * 3 + q])
+            out = out[:, 0:128] + out[:, 128:256] + dot_nt(low, full_ref[s * 3 + q, 0:128])
             for k in range(2):
                 for e in range(2):
                     part = out[(k * 2 + e) * 64 : (k * 2 + e + 1) * 64]
@@ -298,26 +307,71 @@
     corr_ref[...] = jnp.broadcast_to(jnp.sum(spread, axis=0, keepdims=True), corr_ref.shape)
 
 
-def contract(place, choice, mine, theirs, sink, peram, copies):
-    smem = pl.BlockSpec(memory_space=pltpu.SMEM)
-    vmem = pl.BlockSpec(memory_space=pltpu.VMEM)
+SMEM = pl.BlockSpec(memory_space=pltpu.SMEM)
+VMEM = pl.BlockSpec(memory_space=pltpu.VMEM)
+
+
+def call(kernel, name, outs, ins, scratch, micros, args):
     return pl.pallas_call(
-        contract_kernel,
-        out_shape=(
-            jax.ShapeDtypeStruct((2, 2, 64, 64), F32),
-            jax.ShapeDtypeStruct((copies, 128), F32),
+        kernel,
+        out_shape=outs,
+        in_specs=ins,
+        out_specs=jax.tree.map(lambda _: VMEM, outs),
+        scratch_shapes=scratch,
+        compiler_params=pltpu.CompilerParams(vmem_limit_bytes=16 << 20),
+        cost_estimate=pl.CostEstimate(flops=0, bytes_accessed=int(micros * 3.5e6), transcendentals=0),
+        name=name,
+    )(*args)
+
+
+def shape_of(dtype, *dims):
+    return jax.ShapeDtypeStruct(dims, dtype)
+
+
+def prepare(place, choice, peram):
+    count = 3 * choice.shape[0]
+    return call(
+        prepare_kernel,
+        "prepare",
+        (
+            shape_of(BF16, 2, 64, 128),
+            shape_of(BF16, 2, 64, 128),
+            shape_of(BF16, count, 128, 192),
+            shape_of(BF16, count, 256, 128),
         ),
-        in_specs=[smem, smem, vmem, vmem, vmem, vmem],
-        out_specs=(vmem, vmem),
-        scratch_shapes=[
-            pltpu.VMEM((2 * HALF * HALF, 128), F32),
-            pltpu.VMEM((12, 64, 128), F32),
-            pltpu.VMEM((HALF, 128), F32),
-            pltpu.VMEM((HALF * 64, 128), F32),
-        ],
-        compiler_params=pltpu.CompilerParams(vmem_limit_bytes=24 << 20),
-        name="contract",
-    )(place, choice, mine, theirs, sink, peram)
+        [SMEM, SMEM, VMEM],
+        [pltpu.VMEM((count, 64, 128), F32), pltpu.VMEM((HALF, 128), F32)],
+        3,
+        (place, choice, peram),
+    )
+
+
+def first_index(left_r, left_n, mine, theirs):
+    return call(
+        first_index_kernel,
+        "first_index",
+        shape_of(F32, HALF * 64, 128),
+        [VMEM] * 4,
+        [pltpu.VMEM((2 * HALF * HALF, 128), F32)],
+        8,
+        (left_r, left_n, mine, theirs),
+    )
+
+
+def own_rows(place, inner):
+    return call(rows_kernel, "own_rows", shape_of(F32, 2, 2, 64, 64), [SMEM, VMEM], [], 3, (place, inner))
+
+
+def correlate(place, sink, flipped, full, inner, copies):
+    return call(
+        correlate_kernel,
+        "correlate",
+        shape_of(F32, copies, 128),
+        [SMEM, VMEM, VMEM, VMEM, VMEM],
+        [],
+        4,
+        (place, sink, flipped, full, inner),
+    )
 
 
 def swapped(value, axis, mask):
@@ -343,9 +397,12 @@
     part = (keep + got).reshape(run_count, -1, 128)
     own = lax.all_to_all(part, ("z", "yl"), 0, 0, tiled=True).sum(0)
 
+    place = jnp.stack([core, run]).astype(jnp.int32)
+    place, own = lax.optimization_barrier((place, own))
     near = jnp.stack([own, swapped(own, "yh", 1)])
     every = jnp.broadcast_to(own[None], (run_count,) + own.shape)
     mine = lax.all_to_all(every, ("z", "yl"), 0, 0, tiled=True).reshape(-1, 128)
+    left_r, left_n, flipped, full = prepare(place, spin_choice, peram)
     theirs = swapped(mine, "core", 1)
     wider = jnp.concatenate([near, swapped(near, "x", 1)])
     all_times = jnp.concatenate([wider, swapped(wider, "x", 2)])
@@ -354,9 +411,10 @@
     pick = (away_by & 2) * 2 + (away_by & 1) * 2 + (away_by >> 2)
     sink = lax.dynamic_index_in_dim(all_times, pick, 0, keepdims=False)
 
-    place = jnp.stack([core, run]).astype(jnp.int32)
-    rows, corr = contract(place, spin_choice, mine, theirs, sink, peram, space_count)
+    inner = first_index(left_r, left_n, mine, theirs)
+    corr = correlate(place, sink, flipped, full, inner, space_count)
     total = lax.all_to_all(corr, ("z", "yl", "core"), 0, 0, tiled=True).sum(0)
+    rows = own_rows(place, inner)
     correlator = total[: 2 * combos].reshape(1, combos, 2) * corr_factor
     return (rows.reshape(1, 2, 2, nvec * nvec)[0], correlator)
 

time: 84.1 us -> 77.9 us (0.926)
  blocking collectives: 18.8 us -> 0 us
  waiting for transfers between devices: 14 us -> 23.4 us
  starting transfers between devices: 23.3 us -> 30.6 us
  Pallas kernels: 22.2 us -> 16.5 us
    all_to_all x1 -> x0, blocking collectives: 18.8 us -> none  [shards(): own = lax.all_to_all(part, ('z', 'yl'), 0, 0, tiled=True).sum(0)]
    all_to_all x0 -> x1, waiting for transfers between devices: none -> 11.3 us  [shards(): own = lax.all_to_all(part, ('z', 'yl'), 0, 0, tiled=True).sum(0)]
    all_to_all x0 -> x1, starting transfers between devices: none -> 7.57 us  [shards(): own = lax.all_to_all(part, ('z', 'yl'), 0, 0, tiled=True).sum(0)]
    pallas_call x1 -> x4, Pallas kernels: 18 us -> 12.3 us  [call(): pl.pallas_call(kernel, out_shape=outs, in_specs=ins, out_specs=jax.tree.m...]
    ppermute x5, waiting for transfers between devices: 3.9 us -> 1.49 us  [swapped(): return lax.ppermute(value, axis, [(i, i ^ mask) for i in range(count)])]
    all_to_all x1, waiting for transfers between devices: 3.02 us -> 4.33 us  [shards(): mine = lax.all_to_all(every, ('z', 'yl'), 0, 0, tiled=True).reshape(-1, 128)]
    all_to_all x1, waiting for transfers between devices: 7.08 us -> 6.19 us  [shards(): total = lax.all_to_all(corr, ('z', 'yl', 'core'), 0, 0, tiled=True).sum(0)]
  transfers between devices with their start and end apart: 7 -> 8, of which waited for: 4 -> 4; matrix products, arithmetic and copies ran while one was open for 2% -> 2% of each run, Pallas kernels for 3% -> 9%
where the time goes in v2:
time: 77.9 us; the launch traced here: 77.4 us
  starting transfers between devices  30.6 us (39%)
  waiting for transfers between devices  23.4 us (30%)
  Pallas kernels  16.5 us (21%)
  local copies, waits for them, and re-layouts  4.53 us (6%)
  between operations  1.45 us (2%)
  other arithmetic  0.92 us (1%)
    ppermute x5, starting transfers between devices, swapped(): return lax.ppermute(value, axis, [(i, i ^ mask) for i in range(count)])  13.6 us
    pallas_call x4, Pallas kernels, call(): pl.pallas_call(kernel, out_shape=outs, in_specs=ins, out_specs=jax.tree.m...  12.3 us
    all_to_all x1, waiting for transfers between devices, shards(): own = lax.all_to_all(part, ('z', 'yl'), 0, 0, tiled=True).sum(0)  11.3 us
    all_to_all x1, starting transfers between devices, shards(): own = lax.all_to_all(part, ('z', 'yl'), 0, 0, tiled=True).sum(0)  7.57 us
    all_to_all x1, waiting for transfers between devices, shards(): total = lax.all_to_all(corr, ('z', 'yl', 'core'), 0, 0, tiled=True).sum(0)  6.19 us
    all_to_all x1, starting transfers between devices, shards(): total = lax.all_to_all(corr, ('z', 'yl', 'core'), 0, 0, tiled=True).sum(0)  5.96 us
    all_to_all x1, waiting for transfers between devices, shards(): mine = lax.all_to_all(every, ('z', 'yl'), 0, 0, tiled=True).reshape(-1, 128)  4.33 us
    pallas_call x2, Pallas kernels, pair_products(): pl.pallas_call(functools.partial(pair_kernel, factor), out_shape=jax.Shap...  4.2 us
  transfers between devices with their start and end apart: 8, of which 4 were waited for; matrix products, arithmetic and copies ran while one was open for 2% of the time, Pallas kernels for 9%

profile of v2, /device:TPU:1, one launch (start us, length us, event | category | flops | bytes accessed | tf_op | source)
XLA Modules:
  0.0 77.4 jit_solution(17014557610882016708)
XLA Ops:
  0.6 1.0 %copy-done = f32[1,2,3,64,256]{4,3,2,1,0:T(8,128)S(1)} copy-done((f32[1,2,3,64,256]{4,3,2,1,0:T(8,128)S(1)}, f32[1,2,3,64,256]{4,3,2,1,0:T(8,128)}, u32[]{:S(2)}) %copy-start) | copy-done | bytes 393240
  1.6 2.1 %pair_products.3 = f32[512,128]{1,0:T(8,128)S(1)} custom-call(s32[1]{0:T(128)} %bitcast.3.half_ref, f32[2,3,64,256]{3,2,1,0:T(8,128)S(1)} %bitcast.17), custom_call_target="tpu_custom_call" | custom-call | tf_op jit(solution)/shard_map/pair_products/pallas_call | solution.py:95
  3.7 3.3 %collective-permute-start = (f32[512,128]{1,0:T(8,128)S(1)}, f32[512,128]{1,0:T(8,128)S(1)}, u32[]{:S(2)}, u32[]{:S(2)}) collective-permute-start(f32[512,128]{1,0:T(8,128)S(1)} %pair_products.3), channel_id=1, source_target_pairs={{0,1},{1,0},{2,3},{3,2},{4,5},{5,4},{6,7},{7,6},{8,9},{9,8},{10,11... | collective-permute-start | bytes 786440 | tf_op jit(solution)/shard_map/ppermute | solution.py:379
  7.1 2.1 %pair_products.2 = f32[512,128]{1,0:T(8,128)S(1)} custom-call(s32[1]{0:T(128)} %bitcast.half_ref, f32[2,3,64,256]{3,2,1,0:T(8,128)S(1)} %bitcast.18), custom_call_target="tpu_custom_call" | custom-call | tf_op jit(solution)/shard_map/pair_products/pallas_call | solution.py:95
  9.2 0.7 add.28
  9.9 7.6 %all-to-all-start = ((f32[16,32,128]{2,1,0:T(8,128)}), f32[16,32,128]{2,1,0:T(8,128)S(1)}, u32[]{:S(2)}, u32[]{:S(2)}) async-start(f32[16,32,128]{2,1,0:T(8,128)} %bitcast.4), calls=%async_computation | async-start | bytes 524288 | tf_op jit(solution)/shard_map/all_to_all | solution.py:398
  17.6 11.3 %all-to-all-done = f32[16,32,128]{2,1,0:T(8,128)S(1)} async-done(((f32[16,32,128]{2,1,0:T(8,128)}), f32[16,32,128]{2,1,0:T(8,128)S(1)}, u32[]{:S(2)}, u32[]{:S(2)}) %all-to-all-start) | async-done | bytes 262176 | tf_op jit(solution)/shard_map/all_to_all | solution.py:398
  29.0 0.7 broadcast_in_dim.13
  29.7 3.5 %all-to-all-start.1 = ((f32[16,32,128]{2,1,0:T(8,128)}), f32[16,32,128]{2,1,0:T(8,128)S(1)}, u32[]{:S(2)}, u32[]{:S(2)}) async-start(f32[16,32,128]{2,1,0:T(8,128)} %broadcast_in_dim.13), calls=%async_computation.1 | async-start | bytes 524288 | tf_op jit(solution)/shard_map/all_to_all | solution.py:404
  33.2 2.7 %collective-permute-start.2 = (f32[32,128]{1,0:T(8,128)S(1)}, f32[32,128]{1,0:T(8,128)S(1)}, u32[]{:S(2)}, u32[]{:S(2)}) collective-permute-start(f32[32,128]{1,0:T(8,128)S(1)} %reduce_sum.18), channel_id=1, source_target_pairs={{0,128},{128,0},{1,129},{129,1},{2,130},{130,2},{3,131},{131,3},{4... | collective-permute-start | bytes 49160 | tf_op jit(solution)/shard_map/ppermute | solution.py:379
  36.0 1.5 %collective-permute-done.2 = f32[32,128]{1,0:T(8,128)S(1)} collective-permute-done((f32[32,128]{1,0:T(8,128)S(1)}, f32[32,128]{1,0:T(8,128)S(1)}, u32[]{:S(2)}, u32[]{:S(2)}) %collective-permute-start.2) | collective-permute-done | bytes 16416 | tf_op jit(solution)/shard_map/ppermute | solution.py:379
  37.4 1.2 %collective-permute-start.3 = (f32[2,32,128]{2,1,0:T(8,128)S(1)}, f32[2,32,128]{2,1,0:T(8,128)S(1)}, u32[]{:S(2)}, u32[]{:S(2)}) collective-permute-start(f32[2,32,128]{2,1,0:T(8,128)S(1)} %pad_maximum_fusion.1), channel_id=1, source_target_pairs={{0,32},{32,0},{64,96},{96,64},{1,33},{33,1},{65,97},{97,65},{2,34}... | collective-permute-start | bytes 98312 | tf_op jit(solution)/shard_map/ppermute | solution.py:379
  38.6 4.3 %all-to-all-done.1 = f32[16,32,128]{2,1,0:T(8,128)S(1)} async-done(((f32[16,32,128]{2,1,0:T(8,128)}), f32[16,32,128]{2,1,0:T(8,128)S(1)}, u32[]{:S(2)}, u32[]{:S(2)}) %all-to-all-start.1) | async-done | bytes 262176 | tf_op jit(solution)/shard_map/all_to_all | solution.py:404
  43.0 3.3 %collective-permute-start.1 = (f32[512,128]{1,0:T(8,128)S(1)}, f32[512,128]{1,0:T(8,128)S(1)}, u32[]{:S(2)}, u32[]{:S(2)}) collective-permute-start(f32[512,128]{1,0:T(8,128)S(1)} %bitcast.19), channel_id=1, source_target_pairs={{0,1},{1,0},{2,3},{3,2},{4,5},{5,4},{6,7},{7,6},{8,9},{9,8},{10,11... | collective-permute-start | bytes 786440 | tf_op jit(solution)/shard_map/ppermute | solution.py:379
  46.3 3.0 %collective-permute-start.4 = (f32[4,32,128]{2,1,0:T(8,128)S(1)}, f32[4,32,128]{2,1,0:T(8,128)S(1)}, u32[]{:S(2)}, u32[]{:S(2)}) collective-permute-start(f32[4,32,128]{2,1,0:T(8,128)S(1)} %pad_maximum_fusion), channel_id=1, source_target_pairs={{0,64},{32,96},{64,0},{96,32},{1,65},{33,97},{65,1},{97,33},{2,66}... | collective-permute-start | bytes 196616 | tf_op jit(solution)/shard_map/ppermute | solution.py:379
  50.6 0.7 copy-done.2
  51.3 4.1 %prepare.1 = (bf16[2,64,128]{2,1,0:T(8,128)(2,1)S(1)}, bf16[2,64,128]{2,1,0:T(8,128)(2,1)S(1)}, bf16[12,128,192]{2,1,0:T(8,128)(2,1)S(1)}, bf16[12,256,128]{2,1,0:T(8,128)(2,1)S(1)}) custom-call(s32[2]{0:T(128)S(1)} %pad_add_fusion.place_ref, s32[4,3]{1,0:T(4,128)S(1)} %copy-done.2, f32[16,2,64,64]{3,2,1,0:T(8,128)S(1)} %reshape_squeeze.3.peram_ref), custom_call_target="tpu_custom_call" | custom-call | bytes 10500000 | tf_op jit(solution)/shard_map/prepare/pallas_call | solution.py:315
  55.5 4.6 %first_index.1.inner_ref = f32[2048,128]{1,0:T(8,128)S(1)} custom-call(bf16[2,64,128]{2,1,0:T(8,128)(2,1)S(1)} %get-tuple-element.9.left_r_ref, bf16[2,64,128]{2,1,0:T(8,128)(2,1)S(1)} %get-tuple-element.10.left_n_ref, f32[512,128]{1,0:T(8,128)S(1)} %bitcast.20, f32[512,128]{1,0:T(8,128)S(1)} %collective-permute-done.1.theirs_ref), custom_call_target="tpu_custom_call" | custom-call | bytes 28000000 | tf_op jit(solution)/shard_map/first_index/pallas_call | solution.py:315
  60.1 2.7 %correlate.1 = f32[32,128]{1,0:T(8,128)} custom-call(s32[2]{0:T(128)S(1)} %pad_add_fusion.place_ref, f32[32,128]{1,0:T(8,128)S(1)} %fusion.3.sink_ref, bf16[12,128,192]{2,1,0:T(8,128)(2,1)S(1)} %get-tuple-element.12.flipped_ref, bf16[12,256,128]{2,1,0:T(8,128)(2,1)S(1)} %get-tuple-element.13.full_ref, f32[2048,128]{1,0:T(8,128)S(1)} %first_index.1.inner_ref), custom_call_target="tpu_custom_call" | custom-call | bytes 14000000 | tf_op jit(solution)/shard_map/correlate/pallas_call | solution.py:315
  62.8 6.0 %all-to-all-start.2 = ((f32[32,1,128]{2,1,0:T(1,128)}), f32[32,1,128]{2,1,0:T(1,128)S(1)}, u32[]{:S(2)}, u32[]{:S(2)}) async-start(f32[32,1,128]{2,1,0:T(1,128)} %bitcast.11), calls=%async_computation.2 | async-start | bytes 32768 | tf_op jit(solution)/shard_map/all_to_all | solution.py:416
  68.8 0.9 %own_rows.1 = f32[2,2,64,64]{3,2,1,0:T(8,128)S(1)} custom-call(s32[2]{0:T(128)S(1)} %pad_add_fusion.place_ref, f32[2048,128]{1,0:T(8,128)S(1)} %first_index.1.inner_ref), custom_call_target="tpu_custom_call" | custom-call | bytes 10500000 | tf_op jit(solution)/shard_map/own_rows/pallas_call | solution.py:315
  69.7 0.7 broadcast_in_dim_squeeze_reshape.3
  70.4 6.2 %all-to-all-done.2 = f32[32,1,128]{2,1,0:T(1,128)S(1)} async-done(((f32[32,1,128]{2,1,0:T(1,128)}), f32[32,1,128]{2,1,0:T(1,128)S(1)}, u32[]{:S(2)}, u32[]{:S(2)}) %all-to-all-start.2) | async-done | bytes 16416 | tf_op jit(solution)/shard_map/all_to_all | solution.py:416
  76.8 0.7 copy.9
  (19 shorter events, 0.9 us)
Async XLA Ops:
  0.6 1.0 %copy-start = (f32[1,2,3,64,256]{4,3,2,1,0:T(8,128)S(1)}, f32[1,2,3,64,256]{4,3,2,1,0:T(8,128)}, u32[]{:S(2)}) copy-start(f32[1,2,3,64,256]{4,3,2,1,0:T(8,128)} %param.4) | copy-start | bytes 1179652
  1.6 5.4 %copy-start.1 = (f32[1,2,3,64,256]{4,3,2,1,0:T(8,128)S(1)}, f32[1,2,3,64,256]{4,3,2,1,0:T(8,128)}, u32[]{:S(2)}) copy-start(f32[1,2,3,64,256]{4,3,2,1,0:T(8,128)} %param.4) | copy-start | bytes 1179652
  3.7 5.4 %collective-permute-start = (f32[512,128]{1,0:T(8,128)S(1)}, f32[512,128]{1,0:T(8,128)S(1)}, u32[]{:S(2)}, u32[]{:S(2)}) collective-permute-start(f32[512,128]{1,0:T(8,128)S(1)} %pair_products.3), channel_id=1, source_target_pairs={{0,1},{1,0},{2,3},{3,2},{4,5},{5,4},{6,7},{7,6},{8,9},{9,8},{10,11... | collective-permute-start | bytes 786440 | tf_op jit(solution)/shard_map/ppermute | solution.py:379
  9.9 19.0 %all-to-all-start = ((f32[16,32,128]{2,1,0:T(8,128)}), f32[16,32,128]{2,1,0:T(8,128)S(1)}, u32[]{:S(2)}, u32[]{:S(2)}) async-start(f32[16,32,128]{2,1,0:T(8,128)} %bitcast.4), calls=%async_computation | async-start | bytes 524288 | tf_op jit(solution)/shard_map/all_to_all | solution.py:398
  29.0 21.0 %copy-start.3 = (f32[1,16,2,4096]{3,2,1,0:T(2,128)S(1)}, f32[1,16,2,4096]{3,2,1,0:T(2,128)}, u32[]{:S(2)}) copy-start(f32[1,16,2,4096]{3,2,1,0:T(2,128)} %param.5) | copy-start | bytes 1572868
  29.7 13.3 %all-to-all-start.1 = ((f32[16,32,128]{2,1,0:T(8,128)}), f32[16,32,128]{2,1,0:T(8,128)S(1)}, u32[]{:S(2)}, u32[]{:S(2)}) async-start(f32[16,32,128]{2,1,0:T(8,128)} %broadcast_in_dim.13), calls=%async_computation.1 | async-start | bytes 524288 | tf_op jit(solution)/shard_map/all_to_all | solution.py:404
  33.2 4.2 %collective-permute-start.2 = (f32[32,128]{1,0:T(8,128)S(1)}, f32[32,128]{1,0:T(8,128)S(1)}, u32[]{:S(2)}, u32[]{:S(2)}) collective-permute-start(f32[32,128]{1,0:T(8,128)S(1)} %reduce_sum.18), channel_id=1, source_target_pairs={{0,128},{128,0},{1,129},{129,1},{2,130},{130,2},{3,131},{131,3},{4... | collective-permute-start | bytes 49160 | tf_op jit(solution)/shard_map/ppermute | solution.py:379
  37.4 8.9 %collective-permute-start.3 = (f32[2,32,128]{2,1,0:T(8,128)S(1)}, f32[2,32,128]{2,1,0:T(8,128)S(1)}, u32[]{:S(2)}, u32[]{:S(2)}) collective-permute-start(f32[2,32,128]{2,1,0:T(8,128)S(1)} %pad_maximum_fusion.1), channel_id=1, source_target_pairs={{0,32},{32,0},{64,96},{96,64},{1,33},{33,1},{65,97},{97,65},{2,34}... | collective-permute-start | bytes 98312 | tf_op jit(solution)/shard_map/ppermute | solution.py:379
  43.0 12.5 %collective-permute-start.1 = (f32[512,128]{1,0:T(8,128)S(1)}, f32[512,128]{1,0:T(8,128)S(1)}, u32[]{:S(2)}, u32[]{:S(2)}) collective-permute-start(f32[512,128]{1,0:T(8,128)S(1)} %bitcast.19), channel_id=1, source_target_pairs={{0,1},{1,0},{2,3},{3,2},{4,5},{5,4},{6,7},{7,6},{8,9},{9,8},{10,11... | collective-permute-start | bytes 786440 | tf_op jit(solution)/shard_map/ppermute | solution.py:379
  46.3 9.1 %collective-permute-start.4 = (f32[4,32,128]{2,1,0:T(8,128)S(1)}, f32[4,32,128]{2,1,0:T(8,128)S(1)}, u32[]{:S(2)}, u32[]{:S(2)}) collective-permute-start(f32[4,32,128]{2,1,0:T(8,128)S(1)} %pad_maximum_fusion), channel_id=1, source_target_pairs={{0,64},{32,96},{64,0},{96,32},{1,65},{33,97},{65,1},{97,33},{2,66}... | collective-permute-start | bytes 196616 | tf_op jit(solution)/shard_map/ppermute | solution.py:379
  50.6 0.7 copy-start.2
  62.8 13.8 %all-to-all-start.2 = ((f32[32,1,128]{2,1,0:T(1,128)}), f32[32,1,128]{2,1,0:T(1,128)S(1)}, u32[]{:S(2)}, u32[]{:S(2)}) async-start(f32[32,1,128]{2,1,0:T(1,128)} %bitcast.11), calls=%async_computation.2 | async-start | bytes 32768 | tf_op jit(solution)/shard_map/all_to_all | solution.py:416

commit v3 on v2

--- a/solution.py
+++ b/solution.py
@@ -161,19 +161,40 @@
     sign = part_signs((HALF, 128))
     lead_high, lead_low = split(lead)
     conj_high, conj_low = split(lead * sign)
+    cross_high, cross_low = split(swap_parts(lead))
     blank = jnp.zeros((HALF, 64), BF16)
     for g in range(2):
-        here = slice(g * 64, g * 64 + 64)
+        re, im = slice(g * 64, g * 64 + 32), slice(g * 64 + 32, g * 64 + 64)
         there = slice(64 - g * 64, 128 - g * 64)
-        left_r_ref[g, 0:HALF] = jnp.concatenate([-lead_high[:, here], -lead_high[:, here]], axis=1)
-        left_r_ref[g, HALF : 2 * HALF] = jnp.concatenate([-lead_low[:, here], blank], axis=1)
-        left_n_ref[g, 0:HALF] = jnp.concatenate([conj_high[:, there], conj_high[:, there]], axis=1)
-        left_n_ref[g, HALF : 2 * HALF] = jnp.concatenate([conj_low[:, there], blank], axis=1)
-
-
-def first_index_kernel(left_r_ref, left_n_ref, mine_ref, theirs_ref, inner, pairs):
-    for g, from_ref in enumerate((mine_ref, theirs_ref)):
+        none = jnp.zeros((HALF, 32), BF16)
+        for k, rows in enumerate(
+            (
+                (-lead_high[:, re], -lead_high[:, re]),
+                (-lead_high[:, im], -lead_high[:, im]),
+                (-lead_low[:, re], none),
+                (-lead_low[:, im], none),
+            )
+        ):
+            left_r_ref[g, k * HALF : (k + 1) * HALF] = jnp.concatenate(rows, axis=1)
+        for k, (rows, low_rows) in enumerate(
+            (
+                (conj_high[:, there], conj_high[:, there]),
+                (cross_high[:, there], cross_high[:, there]),
+                (conj_low[:, there], blank),
+                (cross_low[:, there], blank),
+            )
+        ):
+            left_n_ref[g, k * HALF : (k + 1) * HALF] = jnp.concatenate([rows, low_rows], axis=1)
+
+
+def first_index_kernel(left_r_ref, left_n_ref, mine_ref, theirs_ref, inner, pairs, turned_ref):
+    for g in range(2):
         base = g * HALF * HALF
+        if g == 0:
+            from_ref = mine_ref
+        else:
+            turned_ref[...] = pltpu.roll(theirs_ref[...], 64, 1)
+            from_ref = turned_ref
         pairs[pl.ds(base, HALF, stride=HALF + 1), :] = jnp.zeros((HALF, 128), F32)
         for j in range(HALF):
             straight = min(STEPS, HALF - 1 - j)
@@ -194,29 +215,40 @@
     sign = part_signs((HALF, 128))
     for g in range(2):
         left_r, left_n = left_r_ref[g], left_n_ref[g]
-        for b in range(0, HALF, 2):
-            right_r, right_n = [], []
-            for e in range(2):
+        here = g * 64
+        for b in range(0, HALF, 4):
+            stacks, packs = [], []
+            for e in range(4):
                 at = (g * HALF + b + e) * HALF
                 value = pairs[at : at + HALF]
-                parts, packs = [], []
-                for one in (value, turned(value, sign)):
-                    high = one.astype(BF16)
-                    low = one - high.astype(F32)
-                    parts.append((high, low.astype(BF16)))
-                    packs.append(jnp.where(wide < 64, pltpu.roll(high.astype(F32), 64, 1), low))
-                right_r.append(jnp.concatenate([parts[0][0], parts[1][0], parts[0][1], parts[1][1]], axis=0))
-                right_n += [packs[0].astype(BF16), (-packs[1]).astype(BF16)]
-            some = dot_nn(left_r, jnp.concatenate(right_r, axis=1))
-            some = some[0:HALF] + some[HALF : 2 * HALF]
-            more = dot_nt(left_n, jnp.concatenate(right_n, axis=0))
-            more = more[0:HALF] + more[HALF : 2 * HALF]
-            for e in range(2):
-                extra = more if e == 0 else pltpu.roll(more, 64, 1)
-                result = some[:, e * 128 : (e + 1) * 128] + jnp.where(wide < 64, extra, 0.0)
-                if g == 1:
-                    result = pltpu.roll(result, 64, 1)
-                inner[pl.ds(g * HALF + b + e, HALF, stride=64), :] = result
+                high = value.astype(BF16)
+                full = high.astype(F32)
+                low = value - full
+                stacks.append(jnp.concatenate([high, low.astype(BF16)], axis=0))
+                if g == 0:
+                    full = pltpu.roll(full, 64, 1)
+                else:
+                    low = pltpu.roll(low, 64, 1)
+                packs.append(jnp.where(wide < 64, full, low).astype(BF16))
+            more = dot_nt(left_n, jnp.concatenate(packs, axis=0))
+            more_re = more[0:HALF] + more[2 * HALF : 3 * HALF]
+            more_im = more[HALF : 2 * HALF] + more[3 * HALF : 4 * HALF]
+            for pair in range(2):
+                some = dot_nn(left_r, jnp.concatenate(stacks[2 * pair : 2 * pair + 2], axis=1))
+                some_re = some[0:HALF] + some[2 * HALF : 3 * HALF]
+                some_im = some[HALF : 2 * HALF] + some[3 * HALF : 4 * HALF]
+                for e in range(2):
+                    at = (2 * pair + e) * 32
+                    columns = slice(e * 128, e * 128 + 128)
+                    result = some_re[:, columns] + turned(some_im[:, columns], sign)
+                    extra_re, extra_im = more_re, more_im
+                    if (here - at) % 128:
+                        extra_re = pltpu.roll(extra_re, (here - at) % 128, 1)
+                    if (here + 32 - at) % 128:
+                        extra_im = pltpu.roll(extra_im, (here + 32 - at) % 128, 1)
+                    extra = jnp.where(wide % 64 < 32, extra_re, extra_im)
+                    result += jnp.where((wide < 64) == (g == 0), extra, 0.0)
+                    inner[pl.ds(g * HALF + b + 2 * pair + e, HALF, stride=64), :] = result
 
 
 def rows_kernel(place_ref, inner_ref, rows_ref):
@@ -300,8 +332,9 @@
                     part = out[(k * 2 + e) * 64 : (k * 2 + e + 1) * 64]
                     acc_re += part * dual[partners[k]][e][0]
                     acc_im += part * dual[partners[k]][e][1]
-        results += [jnp.sum(acc_re, axis=0, keepdims=True), jnp.sum(acc_im, axis=0, keepdims=True)]
-    table = jnp.sum(jnp.concatenate(results, axis=0), axis=1, keepdims=True)
+        results.append((jnp.sum(acc_re, axis=0, keepdims=True), jnp.sum(acc_im, axis=0, keepdims=True)))
+    table = jnp.concatenate([result[part] for part in range(2) for result in results], axis=0)
+    table = jnp.sum(table, axis=1, keepdims=True)
     shape = (2 * combos, 128)
     spread = jnp.where(lax.broadcasted_iota(jnp.int32, shape, 0) == lanes_of(shape), table, 0.0)
     corr_ref[...] = jnp.broadcast_to(jnp.sum(spread, axis=0, keepdims=True), corr_ref.shape)
@@ -334,8 +367,8 @@
         prepare_kernel,
         "prepare",
         (
-            shape_of(BF16, 2, 64, 128),
-            shape_of(BF16, 2, 64, 128),
+            shape_of(BF16, 2, 128, 64),
+            shape_of(BF16, 2, 128, 128),
             shape_of(BF16, count, 128, 192),
             shape_of(BF16, count, 256, 128),
         ),
@@ -352,8 +385,8 @@
         "first_index",
         shape_of(F32, HALF * 64, 128),
         [VMEM] * 4,
-        [pltpu.VMEM((2 * HALF * HALF, 128), F32)],
-        8,
+        [pltpu.VMEM((2 * HALF * HALF, 128), F32), pltpu.VMEM((HALF * STEPS, 128), F32)],
+        5,
         (left_r, left_n, mine, theirs),
     )
 
@@ -395,27 +428,33 @@
     got = swapped(away, "core", 1)
     keep = pair_products(core[None], vec, factor)
     part = (keep + got).reshape(run_count, -1, 128)
-    own = lax.all_to_all(part, ("z", "yl"), 0, 0, tiled=True).sum(0)
-
     place = jnp.stack([core, run]).astype(jnp.int32)
-    place, own = lax.optimization_barrier((place, own))
+    place, part = lax.optimization_barrier((place, part))
+    spread = lax.all_to_all(part, ("z", "yl"), 0, 0, tiled=True)
+    left_r, left_n, flipped, full = prepare(place, spin_choice, peram)
+    spread, left_r = lax.optimization_barrier((spread, left_r))
+    own = spread.sum(0)
+
+    every = jnp.broadcast_to(own[None], (run_count,) + own.shape)
     near = jnp.stack([own, swapped(own, "yh", 1)])
-    every = jnp.broadcast_to(own[None], (run_count,) + own.shape)
-    mine = lax.all_to_all(every, ("z", "yl"), 0, 0, tiled=True).reshape(-1, 128)
-    left_r, left_n, flipped, full = prepare(place, spin_choice, peram)
+    mine = lax.all_to_all(every, ("z", "yl"), 0, 0, tiled=True)
+    side = swapped(near, "x", 1)
+    mine, side = lax.optimization_barrier((mine, side))
+    mine = mine.reshape(-1, 128)
+    wider = jnp.concatenate([near, side])
     theirs = swapped(mine, "core", 1)
-    wider = jnp.concatenate([near, swapped(near, "x", 1)])
-    all_times = jnp.concatenate([wider, swapped(wider, "x", 2)])
+    inner = first_index(left_r, left_n, mine, theirs)
+    last = swapped(wider, "x", 2)
+    last, inner = lax.optimization_barrier((last, inner))
+    all_times = jnp.concatenate([wider, last])
     now = lax.axis_index("yh") * lax.axis_size("x") + lax.axis_index("x")
     away_by = now ^ ((now + shift_steps[0]) % 8)
     pick = (away_by & 2) * 2 + (away_by & 1) * 2 + (away_by >> 2)
     sink = lax.dynamic_index_in_dim(all_times, pick, 0, keepdims=False)
-
-    inner = first_index(left_r, left_n, mine, theirs)
     corr = correlate(place, sink, flipped, full, inner, space_count)
     total = lax.all_to_all(corr, ("z", "yl", "core"), 0, 0, tiled=True).sum(0)
     rows = own_rows(place, inner)
-    correlator = total[: 2 * combos].reshape(1, combos, 2) * corr_factor
+    correlator = jnp.transpose((total[: 2 * combos] * corr_factor).reshape(1, 2, combos), (0, 2, 1))
     return (rows.reshape(1, 2, 2, nvec * nvec)[0], correlator)
 
 

time: 77.9 us -> 71.5 us (0.918)
  waiting for transfers between devices: 23.4 us -> 18.6 us
  Pallas kernels: 16.5 us -> 15.5 us
    all_to_all x2, waiting for transfers between devices: 15.7 us -> 9.04 us  [the longest x1 6.56 us: shards(): spread = lax.all_to_all(part, ('z', 'yl'), 0, 0, tiled=True)]
    ppermute x5, waiting for transfers between devices: 1.49 us -> 3.32 us  [swapped(): return lax.ppermute(value, axis, [(i, i ^ mask) for i in range(count)])]
    unnamed x9 -> x8, local copies, waits for them, and re-layouts: 2.34 us -> 1.05 us
    pallas_call x4, Pallas kernels: 12.3 us -> 11.3 us  [call(): pl.pallas_call(kernel, out_shape=outs, in_specs=ins, out_specs=jax.tree.m...]
  transfers between devices with their start and end apart: 8 -> 8, of which waited for: 4 -> 5; matrix products, arithmetic and copies ran while one was open for 2% -> 2% of each run, Pallas kernels for 9% -> 15%
where the time goes in v3:
time: 71.5 us; the launch traced here: 71.1 us
  starting transfers between devices  30.9 us (43%)
  waiting for transfers between devices  18.6 us (26%)
  Pallas kernels  15.5 us (22%)
  local copies, waits for them, and re-layouts  3.8 us (5%)
  between operations  1.44 us (2%)
  other arithmetic  0.94 us (1%)
    ppermute x5, starting transfers between devices, swapped(): return lax.ppermute(value, axis, [(i, i ^ mask) for i in range(count)])  13.3 us
    pallas_call x4, Pallas kernels, call(): pl.pallas_call(kernel, out_shape=outs, in_specs=ins, out_specs=jax.tree.m...  11.3 us
    all_to_all x1, starting transfers between devices, shards(): spread = lax.all_to_all(part, ('z', 'yl'), 0, 0, tiled=True)  7.57 us
    all_to_all x1, waiting for transfers between devices, shards(): spread = lax.all_to_all(part, ('z', 'yl'), 0, 0, tiled=True)  6.56 us
    all_to_all x1, starting transfers between devices, shards(): total = lax.all_to_all(corr, ('z', 'yl', 'core'), 0, 0, tiled=True).sum(0)  6.49 us
    all_to_all x1, waiting for transfers between devices, shards(): total = lax.all_to_all(corr, ('z', 'yl', 'core'), 0, 0, tiled=True).sum(0)  6.19 us
    pallas_call x2, Pallas kernels, pair_products(): pl.pallas_call(functools.partial(pair_kernel, factor), out_shape=jax.Shap...  4.18 us
    all_to_all x1, starting transfers between devices, shards(): mine = lax.all_to_all(every, ('z', 'yl'), 0, 0, tiled=True)  3.53 us
  transfers between devices with their start and end apart: 8, of which 5 were waited for; matrix products, arithmetic and copies ran while one was open for 2% of the time, Pallas kernels for 15%

profile of v3, /device:TPU:1, one launch (start us, length us, event | category | flops | bytes accessed | tf_op | source)
XLA Modules:
  0.0 71.1 jit_solution(11305988928740088388)
XLA Ops:
  0.6 1.0 %copy-done = f32[1,2,3,64,256]{4,3,2,1,0:T(8,128)S(1)} copy-done((f32[1,2,3,64,256]{4,3,2,1,0:T(8,128)S(1)}, f32[1,2,3,64,256]{4,3,2,1,0:T(8,128)}, u32[]{:S(2)}) %copy-start) | copy-done | bytes 393240
  1.6 2.1 %pair_products.3 = f32[512,128]{1,0:T(8,128)S(1)} custom-call(s32[1]{0:T(128)} %bitcast.3.half_ref, f32[2,3,64,256]{3,2,1,0:T(8,128)S(1)} %bitcast.18), custom_call_target="tpu_custom_call" | custom-call | tf_op jit(solution)/shard_map/pair_products/pallas_call | solution.py:95
  3.7 3.3 %collective-permute-start = (f32[512,128]{1,0:T(8,128)S(1)}, f32[512,128]{1,0:T(8,128)S(1)}, u32[]{:S(2)}, u32[]{:S(2)}) collective-permute-start(f32[512,128]{1,0:T(8,128)S(1)} %pair_products.3), channel_id=1, source_target_pairs={{0,1},{1,0},{2,3},{3,2},{4,5},{5,4},{6,7},{7,6},{8,9},{9,8},{10,11... | collective-permute-start | bytes 786440 | tf_op jit(solution)/shard_map/ppermute | solution.py:412
  7.1 2.1 %pair_products.2 = f32[512,128]{1,0:T(8,128)S(1)} custom-call(s32[1]{0:T(128)} %bitcast.half_ref, f32[2,3,64,256]{3,2,1,0:T(8,128)S(1)} %bitcast.19), custom_call_target="tpu_custom_call" | custom-call | tf_op jit(solution)/shard_map/pair_products/pallas_call | solution.py:95
  9.3 0.8 %add.28 = f32[512,128]{1,0:T(8,128)} add(f32[512,128]{1,0:T(8,128)S(1)} %pair_products.2, f32[512,128]{1,0:T(8,128)S(1)} %collective-permute-done) | non-fusion elementwise | flops 65536 | bytes 786432 | tf_op jit(solution)/shard_map/add | solution.py:430
  10.0 7.6 %all-to-all-start = ((f32[16,32,128]{2,1,0:T(8,128)}), f32[16,32,128]{2,1,0:T(8,128)S(1)}, u32[]{:S(2)}, u32[]{:S(2)}) async-start(f32[16,32,128]{2,1,0:T(8,128)} %bitcast.4), calls=%async_computation | async-start | bytes 524288 | tf_op jit(solution)/shard_map/all_to_all | solution.py:433
  18.3 4.2 %prepare.1 = (bf16[2,128,64]{2,1,0:T(8,128)(2,1)S(1)}, bf16[2,128,128]{2,1,0:T(8,128)(2,1)S(1)}, bf16[12,128,192]{2,1,0:T(8,128)(2,1)S(1)}, bf16[12,256,128]{2,1,0:T(8,128)(2,1)S(1)}) custom-call(s32[2]{0:T(128)S(1)} %pad_add_fusion.place_ref, s32[4,3]{1,0:T(4,128)S(1)} %copy-done.2, f32[16,2,64,64]{3,2,1,0:T(8,128)S(1)} %reshape_squeeze.3.peram_ref), custom_call_target="tpu_custom_call" | custom-call | bytes 10500000 | tf_op jit(solution)/shard_map/prepare/pallas_call | solution.py:348
  22.4 6.6 %all-to-all-done = f32[16,32,128]{2,1,0:T(8,128)S(1)} async-done(((f32[16,32,128]{2,1,0:T(8,128)}), f32[16,32,128]{2,1,0:T(8,128)S(1)}, u32[]{:S(2)}, u32[]{:S(2)}) %all-to-all-start) | async-done | bytes 262176 | tf_op jit(solution)/shard_map/all_to_all | solution.py:433
  29.0 0.7 %broadcast_in_dim.5 = f32[16,32,128]{2,1,0:T(8,128)} broadcast(f32[32,128]{1,0:T(8,128)S(1)} %reduce_sum.18), dimensions={1,2} | broadcast | bytes 278528 | tf_op jit(solution)/shard_map/broadcast_in_dim | solution.py:438
  29.8 3.5 %all-to-all-start.1 = ((f32[16,32,128]{2,1,0:T(8,128)}), f32[16,32,128]{2,1,0:T(8,128)S(1)}, u32[]{:S(2)}, u32[]{:S(2)}) async-start(f32[16,32,128]{2,1,0:T(8,128)} %broadcast_in_dim.5), calls=%async_computation.1 | async-start | bytes 524288 | tf_op jit(solution)/shard_map/all_to_all | solution.py:440
  33.3 2.7 %collective-permute-start.1 = (f32[32,128]{1,0:T(8,128)S(1)}, f32[32,128]{1,0:T(8,128)S(1)}, u32[]{:S(2)}, u32[]{:S(2)}) collective-permute-start(f32[32,128]{1,0:T(8,128)S(1)} %reduce_sum.18), channel_id=1, source_target_pairs={{0,128},{128,0},{1,129},{129,1},{2,130},{130,2},{3,131},{131,3},{4... | collective-permute-start | bytes 49160 | tf_op jit(solution)/shard_map/ppermute | solution.py:412
  36.0 1.5 %collective-permute-done.1 = f32[32,128]{1,0:T(8,128)S(1)} collective-permute-done((f32[32,128]{1,0:T(8,128)S(1)}, f32[32,128]{1,0:T(8,128)S(1)}, u32[]{:S(2)}, u32[]{:S(2)}) %collective-permute-start.1) | collective-permute-done | bytes 16416 | tf_op jit(solution)/shard_map/ppermute | solution.py:412
  37.5 1.2 %collective-permute-start.2 = (f32[2,32,128]{2,1,0:T(8,128)S(1)}, f32[2,32,128]{2,1,0:T(8,128)S(1)}, u32[]{:S(2)}, u32[]{:S(2)}) collective-permute-start(f32[2,32,128]{2,1,0:T(8,128)S(1)} %pad_maximum_fusion.1), channel_id=1, source_target_pairs={{0,32},{32,0},{64,96},{96,64},{1,33},{33,1},{65,97},{97,65},{2,34}... | collective-permute-start | bytes 98312 | tf_op jit(solution)/shard_map/ppermute | solution.py:412
  38.7 1.9 %collective-permute-done.2 = f32[2,32,128]{2,1,0:T(8,128)S(1)} collective-permute-done((f32[2,32,128]{2,1,0:T(8,128)S(1)}, f32[2,32,128]{2,1,0:T(8,128)S(1)}, u32[]{:S(2)}, u32[]{:S(2)}) %collective-permute-start.2) | collective-permute-done | bytes 32800 | tf_op jit(solution)/shard_map/ppermute | solution.py:412
  40.5 2.5 %all-to-all-done.1 = f32[16,32,128]{2,1,0:T(8,128)S(1)} async-done(((f32[16,32,128]{2,1,0:T(8,128)}), f32[16,32,128]{2,1,0:T(8,128)S(1)}, u32[]{:S(2)}, u32[]{:S(2)}) %all-to-all-start.1) | async-done | bytes 262176 | tf_op jit(solution)/shard_map/all_to_all | solution.py:440
  43.0 3.3 %collective-permute-start.4 = (f32[512,128]{1,0:T(8,128)S(1)}, f32[512,128]{1,0:T(8,128)S(1)}, u32[]{:S(2)}, u32[]{:S(2)}) collective-permute-start(f32[512,128]{1,0:T(8,128)S(1)} %bitcast.20), channel_id=1, source_target_pairs={{0,1},{1,0},{2,3},{3,2},{4,5},{5,4},{6,7},{7,6},{8,9},{9,8},{10,11... | collective-permute-start | bytes 786440 | tf_op jit(solution)/shard_map/ppermute | solution.py:412
  46.4 2.7 %collective-permute-start.3 = (f32[4,32,128]{2,1,0:T(8,128)S(1)}, f32[4,32,128]{2,1,0:T(8,128)S(1)}, u32[]{:S(2)}, u32[]{:S(2)}) collective-permute-start(f32[4,32,128]{2,1,0:T(8,128)S(1)} %pad_maximum_fusion), channel_id=1, source_target_pairs={{0,64},{32,96},{64,0},{96,32},{1,65},{33,97},{65,1},{97,33},{2,66}... | collective-permute-start | bytes 196616 | tf_op jit(solution)/shard_map/ppermute | solution.py:412
  49.8 3.6 %first_index.1.inner_ref = f32[2048,128]{1,0:T(8,128)S(1)} custom-call(bf16[2,128,64]{2,1,0:T(8,128)(2,1)S(1)} %get-tuple-element.19.left_r_ref, bf16[2,128,128]{2,1,0:T(8,128)(2,1)S(1)} %get-tuple-element.20.left_n_ref, f32[512,128]{1,0:T(8,128)S(1)} %bitcast.21, f32[512,128]{1,0:T(8,128)S(1)} %collective-permute-done.4.theirs_ref), custom_call_target="tpu_custom_call" | custom-call | bytes 17500000 | tf_op jit(solution)/shard_map/first_index/pallas_call | solution.py:348
  53.4 2.7 %correlate.1 = f32[32,128]{1,0:T(8,128)} custom-call(s32[2]{0:T(128)S(1)} %pad_add_fusion.place_ref, f32[32,128]{1,0:T(8,128)S(1)} %fusion.3.sink_ref, bf16[12,128,192]{2,1,0:T(8,128)(2,1)S(1)} %get-tuple-element.24.flipped_ref, bf16[12,256,128]{2,1,0:T(8,128)(2,1)S(1)} %get-tuple-element.25.full_ref, f32[2048,128]{1,0:T(8,128)S(1)} %first_index.1.inner_ref), custom_call_target="tpu_custom_call" | custom-call | bytes 14000000 | tf_op jit(solution)/shard_map/correlate/pallas_call | solution.py:348
  56.0 6.5 %all-to-all-start.2 = ((f32[32,1,128]{2,1,0:T(1,128)}), f32[32,1,128]{2,1,0:T(1,128)S(1)}, u32[]{:S(2)}, u32[]{:S(2)}) async-start(f32[32,1,128]{2,1,0:T(1,128)} %bitcast.11), calls=%async_computation.2 | async-start | bytes 32768 | tf_op jit(solution)/shard_map/all_to_all | solution.py:455
  62.5 0.9 %own_rows.1 = f32[2,2,64,64]{3,2,1,0:T(8,128)S(1)} custom-call(s32[2]{0:T(128)S(1)} %pad_add_fusion.place_ref, f32[2048,128]{1,0:T(8,128)S(1)} %first_index.1.inner_ref), custom_call_target="tpu_custom_call" | custom-call | bytes 10500000 | tf_op jit(solution)/shard_map/own_rows/pallas_call | solution.py:348
  63.5 0.7 %broadcast_in_dim_squeeze_reshape.3 = f32[1,2,2,4096]{3,2,1,0:T(2,128)} reshape(f32[2,2,64,64]{3,2,1,0:T(8,128)S(1)} %own_rows.1) | data formatting | bytes 131072 | tf_op jit(solution)/shard_map/broadcast_in_dim;squeeze;reshape | solution.py:468
  64.2 6.2 %all-to-all-done.2 = f32[32,1,128]{2,1,0:T(1,128)S(1)} async-done(((f32[32,1,128]{2,1,0:T(1,128)}), f32[32,1,128]{2,1,0:T(1,128)S(1)}, u32[]{:S(2)}, u32[]{:S(2)}) %all-to-all-start.2) | async-done | bytes 16416 | tf_op jit(solution)/shard_map/all_to_all | solution.py:455
  70.5 0.6 mul.27
  (18 shorter events, 0.9 us)
Async XLA Ops:
  0.6 1.0 %copy-start = (f32[1,2,3,64,256]{4,3,2,1,0:T(8,128)S(1)}, f32[1,2,3,64,256]{4,3,2,1,0:T(8,128)}, u32[]{:S(2)}) copy-start(f32[1,2,3,64,256]{4,3,2,1,0:T(8,128)} %param.4) | copy-start | bytes 1179652
  1.6 5.4 %copy-start.1 = (f32[1,2,3,64,256]{4,3,2,1,0:T(8,128)S(1)}, f32[1,2,3,64,256]{4,3,2,1,0:T(8,128)}, u32[]{:S(2)}) copy-start(f32[1,2,3,64,256]{4,3,2,1,0:T(8,128)} %param.4) | copy-start | bytes 1179652
  3.7 5.5 %collective-permute-start = (f32[512,128]{1,0:T(8,128)S(1)}, f32[512,128]{1,0:T(8,128)S(1)}, u32[]{:S(2)}, u32[]{:S(2)}) collective-permute-start(f32[512,128]{1,0:T(8,128)S(1)} %pair_products.3), channel_id=1, source_target_pairs={{0,1},{1,0},{2,3},{3,2},{4,5},{5,4},{6,7},{7,6},{8,9},{9,8},{10,11... | collective-permute-start | bytes 786440 | tf_op jit(solution)/shard_map/ppermute | solution.py:412
  9.2 8.3 %copy-start.3 = (f32[1,16,2,4096]{3,2,1,0:T(2,128)S(1)}, f32[1,16,2,4096]{3,2,1,0:T(2,128)}, u32[]{:S(2)}) copy-start(f32[1,16,2,4096]{3,2,1,0:T(2,128)} %param.5) | copy-start | bytes 1572868
  10.0 19.0 %all-to-all-start = ((f32[16,32,128]{2,1,0:T(8,128)}), f32[16,32,128]{2,1,0:T(8,128)S(1)}, u32[]{:S(2)}, u32[]{:S(2)}) async-start(f32[16,32,128]{2,1,0:T(8,128)} %bitcast.4), calls=%async_computation | async-start | bytes 524288 | tf_op jit(solution)/shard_map/all_to_all | solution.py:433
  17.6 0.7 copy-start.2
  29.8 13.3 %all-to-all-start.1 = ((f32[16,32,128]{2,1,0:T(8,128)}), f32[16,32,128]{2,1,0:T(8,128)S(1)}, u32[]{:S(2)}, u32[]{:S(2)}) async-start(f32[16,32,128]{2,1,0:T(8,128)} %broadcast_in_dim.5), calls=%async_computation.1 | async-start | bytes 524288 | tf_op jit(solution)/shard_map/all_to_all | solution.py:440
  33.3 4.2 %collective-permute-start.1 = (f32[32,128]{1,0:T(8,128)S(1)}, f32[32,128]{1,0:T(8,128)S(1)}, u32[]{:S(2)}, u32[]{:S(2)}) collective-permute-start(f32[32,128]{1,0:T(8,128)S(1)} %reduce_sum.18), channel_id=1, source_target_pairs={{0,128},{128,0},{1,129},{129,1},{2,130},{130,2},{3,131},{131,3},{4... | collective-permute-start | bytes 49160 | tf_op jit(solution)/shard_map/ppermute | solution.py:412
  37.5 3.1 %collective-permute-start.2 = (f32[2,32,128]{2,1,0:T(8,128)S(1)}, f32[2,32,128]{2,1,0:T(8,128)S(1)}, u32[]{:S(2)}, u32[]{:S(2)}) collective-permute-start(f32[2,32,128]{2,1,0:T(8,128)S(1)} %pad_maximum_fusion.1), channel_id=1, source_target_pairs={{0,32},{32,0},{64,96},{96,64},{1,33},{33,1},{65,97},{97,65},{2,34}... | collective-permute-start | bytes 98312 | tf_op jit(solution)/shard_map/ppermute | solution.py:412
  43.0 6.8 %collective-permute-start.4 = (f32[512,128]{1,0:T(8,128)S(1)}, f32[512,128]{1,0:T(8,128)S(1)}, u32[]{:S(2)}, u32[]{:S(2)}) collective-permute-start(f32[512,128]{1,0:T(8,128)S(1)} %bitcast.20), channel_id=1, source_target_pairs={{0,1},{1,0},{2,3},{3,2},{4,5},{5,4},{6,7},{7,6},{8,9},{9,8},{10,11... | collective-permute-start | bytes 786440 | tf_op jit(solution)/shard_map/ppermute | solution.py:412
  46.4 7.0 %collective-permute-start.3 = (f32[4,32,128]{2,1,0:T(8,128)S(1)}, f32[4,32,128]{2,1,0:T(8,128)S(1)}, u32[]{:S(2)}, u32[]{:S(2)}) collective-permute-start(f32[4,32,128]{2,1,0:T(8,128)S(1)} %pad_maximum_fusion), channel_id=1, source_target_pairs={{0,64},{32,96},{64,0},{96,32},{1,65},{33,97},{65,1},{97,33},{2,66}... | collective-permute-start | bytes 196616 | tf_op jit(solution)/shard_map/ppermute | solution.py:412
  56.0 14.4 %all-to-all-start.2 = ((f32[32,1,128]{2,1,0:T(1,128)}), f32[32,1,128]{2,1,0:T(1,128)S(1)}, u32[]{:S(2)}, u32[]{:S(2)}) async-start(f32[32,1,128]{2,1,0:T(1,128)} %bitcast.11), calls=%async_computation.2 | async-start | bytes 32768 | tf_op jit(solution)/shard_map/all_to_all | solution.py:455

commit v4 on v3

v4 whole, which is shorter than its diff:
```python
import functools
import math

import jax
import jax.numpy as jnp
from jax import lax
from jax.experimental import pallas as pl
from jax.experimental.pallas import tpu as pltpu
from jax.sharding import Mesh
from jax.sharding import PartitionSpec as P

F32 = jnp.float32
BF16 = jnp.bfloat16
HALF = 32
STEPS = 16
LEAD = (1, 0, 2)
SMEM = pl.BlockSpec(memory_space=pltpu.SMEM)
VMEM = pl.BlockSpec(memory_space=pltpu.VMEM)


def split(value):
    high = value.astype(BF16)
    return high, (value - high.astype(F32)).astype(BF16)


def dot_nn(left, right):
    return lax.dot_general(left, right, (((1,), (0,)), ((), ())), preferred_element_type=F32)


def dot_nt(left, right):
    return lax.dot_general(left, right, (((1,), (1,)), ((), ())), preferred_element_type=F32)


def dot_tn(left, right):
    return lax.dot_general(left, right, (((0,), (0,)), ((), ())), preferred_element_type=F32)


def lanes_of(shape):
    return lax.broadcasted_iota(jnp.int32, shape, 1)


def pair_kernel(factor, half_ref, vec_ref, *refs):
    *so_far, out_ref, ext, lead, cross_high, cross_low = refs
    half = half_ref[0]
    own = pl.multiple_of(half * HALF, HALF)
    other = pl.multiple_of((1 - half) * HALF, HALF)
    for part in range(2):
        for colour in range(3):
            ext[part * 3 + colour, 0:HALF] = vec_ref[part, colour, pl.ds(own, HALF), :]
            ext[part * 3 + colour, HALF : HALF + STEPS] = vec_ref[part, colour, pl.ds(own, STEPS), :]
    sites = vec_ref.shape[3]
    for colour in range(3):
        at = colour * 2 * sites
        own_re, own_im = ext[colour, 0:HALF], ext[3 + colour, 0:HALF]
        oth_re = vec_ref[0, colour, pl.ds(other, HALF), :]
        oth_im = vec_ref[1, colour, pl.ds(other, HALF), :]
        for place, value in enumerate(
            (
                (own_re, -own_im),
                (own_im, own_re),
                (oth_re, -oth_im),
                (oth_im, oth_re),
            )
        ):
            for side in range(2):
                high, low = split(value[side])
                columns = slice(at + side * sites, at + (side + 1) * sites)
                lead[place * HALF : (place + 1) * HALF, columns] = high
                lead[128 + place * HALF : 128 + (place + 1) * HALF, columns] = low
    first, second = None, None
    for colour in range(3):
        one, two = (colour + 1) % 3, (colour + 2) % 3
        for step in range(1, STEPS + 1):
            here = slice((step - 1) * HALF, step * HALF)
            one_re, one_im = ext[one, 0:HALF], ext[3 + one, 0:HALF]
            two_re, two_im = ext[two, 0:HALF], ext[3 + two, 0:HALF]
            one_re2, one_im2 = ext[one, step : step + HALF], ext[3 + one, step : step + HALF]
            two_re2, two_im2 = ext[two, step : step + HALF], ext[3 + two, step : step + HALF]
            re = (one_re * two_re2 - one_im * two_im2) - (two_re * one_re2 - two_im * one_im2)
            im = (one_re * two_im2 + one_im * two_re2) - (two_re * one_im2 + two_im * one_re2)
            for side, value in enumerate((re, im)):
                high, low = split(value)
                columns = slice(side * sites, (side + 1) * sites)
                cross_high[colour, here, columns] = high
                cross_low[colour, here, columns] = low
        columns = slice(colour * 2 * sites, (colour + 1) * 2 * sites)
        more = dot_nt(cross_high[colour], lead[:, columns])
        first = more if first is None else first + more
        more = dot_nt(cross_low[colour], lead[0:128, columns])
        second = more if second is None else second + more
    total = (first[:, 0:128] + first[:, 128:256] + second) * (-factor)
    for step in range(STEPS):
        places = pl.ds(step, HALF, stride=STEPS)
        value = total[step * HALF : (step + 1) * HALF]
        out_ref[places, :] = value + so_far[0][places, :] if so_far else value


def pair_products(half, vec, factor, *so_far):
    sites = vec.shape[3]
    return pl.pallas_call(
        functools.partial(pair_kernel, factor),
        out_shape=jax.ShapeDtypeStruct((HALF * STEPS, 128), F32),
        in_specs=[SMEM] + [VMEM] * (1 + len(so_far)),
        out_specs=VMEM,
        scratch_shapes=[
            pltpu.VMEM((6, HALF + STEPS, sites), F32),
            pltpu.VMEM((256, 6 * sites), BF16),
            pltpu.VMEM((3, HALF * STEPS, 2 * sites), BF16),
            pltpu.VMEM((3, HALF * STEPS, 2 * sites), BF16),
        ],
        compiler_params=pltpu.CompilerParams(vmem_limit_bytes=10 << 20),
        name="pair_products",
    )(half, vec, *so_far)


def swap_parts(value):
    lane = lanes_of(value.shape)
    return jnp.where(lane % 64 < 32, pltpu.roll(value, 96, 1), pltpu.roll(value, 32, 1))


def turned(value, sign):
    return -swap_parts(value) * sign


def part_signs(shape):
    return jnp.where(lanes_of(shape) % 64 < 32, 1.0, -1.0)


def prepare_kernel(place_ref, choice_ref, peram_ref, left_r_ref, left_n_ref, flipped_ref, full_ref, quark, weights):
    core, run = place_ref[0], place_ref[1]
    first = core == 0
    combos = choice_ref.shape[0]
    plain = part_signs((64, 128))
    for s in range(combos):
        for q in range(3):
            spin = choice_ref[s, q]
            parts = []
            for part in range(2):
                top = peram_ref[spin, part, pl.ds(pl.multiple_of(core * HALF, HALF), HALF), :]
                low = peram_ref[spin, part, pl.ds(pl.multiple_of((1 - core) * HALF, HALF), HALF), :]
                both = jnp.concatenate([top, low], axis=0)
                left, right = both[:, 0:HALF], both[:, HALF : 2 * HALF]
                parts.append((jnp.where(first, left, right), jnp.where(first, right, left)))
            (re_own, re_oth), (im_own, im_oth) = parts
            value = jnp.concatenate([re_own, im_own, re_oth, im_oth], axis=1)
            quark[s * 3 + q] = value
            high, low = split(value.T)
            flipped_ref[s, q * 128 : (q + 1) * 128] = jnp.concatenate([high, high, low], axis=1)
            full_high, full_low = split(jnp.concatenate([value * plain, swap_parts(value)], axis=0))
            full_ref[s * 3 + q, 0:128] = jnp.concatenate([full_high, full_high], axis=1)
            full_ref[s * 3 + q, 128:256] = jnp.concatenate([full_low, jnp.zeros_like(full_low)], axis=1)

    for s in range(combos):
        for slot in range(3):
            for e in range(2):
                row = s * 6 + slot * 2 + e
                weights[row : row + 1] = quark[s * 3 + LEAD[slot], pl.ds(2 * run + e, 1), :]
    tail = 6 * combos
    shape = (HALF - tail, 128)
    lane, row = lanes_of(shape), lax.broadcasted_iota(jnp.int32, shape, 0)
    number = 4 * run + 2 * core + row
    in_own = (number >= HALF) == (core == 1)
    lit = (number % HALF + jnp.where(in_own, 0, 64)) == lane
    weights[tail:HALF] = jnp.where(lit & (row < 2), 1.0, 0.0)

    lead = weights[...]
    sign = part_signs((HALF, 128))
    lead_high, lead_low = split(lead)
    conj_high, conj_low = split(lead * sign)
    cross_high, cross_low = split(swap_parts(lead))
    blank = jnp.zeros((HALF, 64), BF16)
    for g in range(2):
        re, im = slice(g * 64, g * 64 + 32), slice(g * 64 + 32, g * 64 + 64)
        there = slice(64 - g * 64, 128 - g * 64)
        none = jnp.zeros((HALF, 32), BF16)
        for k, rows in enumerate(
            (
                (-lead_high[:, re], -lead_high[:, re]),
                (-lead_high[:, im], -lead_high[:, im]),
                (-lead_low[:, re], none),
                (-lead_low[:, im], none),
            )
        ):
            left_r_ref[g, k * HALF : (k + 1) * HALF] = jnp.concatenate(rows, axis=1)
        for k, (rows, low_rows) in enumerate(
            (
                (conj_high[:, there], conj_high[:, there]),
                (cross_high[:, there], cross_high[:, there]),
                (conj_low[:, there], blank),
                (cross_low[:, there], blank),
            )
        ):
            left_n_ref[g, k * HALF : (k + 1) * HALF] = jnp.concatenate([rows, low_rows], axis=1)


def first_index_kernel(g, left_r_ref, left_n_ref, from_ref, inner, picked_ref, pairs, *turned_refs):
    if g == 1:
        (turned_ref,) = turned_refs
        turned_ref[...] = pltpu.roll(from_ref[...], 64, 1)
        from_ref = turned_ref
    pairs[pl.ds(0, HALF, stride=HALF + 1), :] = jnp.zeros((HALF, 128), F32)
    for j in range(HALF):
        straight = min(STEPS, HALF - 1 - j)
        at = j * HALF
        if straight:
            pairs[at + j + 1 : at + j + 1 + straight] = from_ref[j * STEPS : j * STEPS + straight]
        if straight < STEPS:
            pairs[at : at + STEPS - straight] = from_ref[j * STEPS + straight : (j + 1) * STEPS]
    for j in range(HALF):
        count = STEPS - 1
        straight = min(count, HALF - 1 - j)
        if straight:
            pairs[pl.ds((j + 1) * HALF + j, straight, stride=HALF), :] = -from_ref[j * STEPS : j * STEPS + straight]
        if straight < count:
            pairs[pl.ds(j, count - straight, stride=HALF), :] = -from_ref[j * STEPS + straight : j * STEPS + count]

    wide = lanes_of((HALF, 128))
    sign = part_signs((HALF, 128))
    left_r, left_n = left_r_ref[g], left_n_ref[g]
    here = g * 64
    for b in range(0, HALF, 4):
        stacks, packs = [], []
        for e in range(4):
            at = (b + e) * HALF
            value = pairs[at : at + HALF]
            high = value.astype(BF16)
            full = high.astype(F32)
            low = value - full
            stacks.append(jnp.concatenate([high, low.astype(BF16)], axis=0))
            if g == 0:
                full = pltpu.roll(full, 64, 1)
            else:
                low = pltpu.roll(low, 64, 1)
            packs.append(jnp.where(wide < 64, full, low).astype(BF16))
        more = dot_nt(left_n, jnp.concatenate(packs, axis=0))
        more_re = more[0:HALF] + more[2 * HALF : 3 * HALF]
        more_im = more[HALF : 2 * HALF] + more[3 * HALF : 4 * HALF]
        for pair in range(2):
            some = dot_nn(left_r, jnp.concatenate(stacks[2 * pair : 2 * pair + 2], axis=1))
            some_re = some[0:HALF] + some[2 * HALF : 3 * HALF]
            some_im = some[HALF : 2 * HALF] + some[3 * HALF : 4 * HALF]
            for e in range(2):
                at = (2 * pair + e) * 32
                columns = slice(e * 128, e * 128 + 128)
                result = some_re[:, columns] + turned(some_im[:, columns], sign)
                extra_re, extra_im = more_re, more_im
                if (here - at) % 128:
                    extra_re = pltpu.roll(extra_re, (here - at) % 128, 1)
                if (here + 32 - at) % 128:
                    extra_im = pltpu.roll(extra_im, (here + 32 - at) % 128, 1)
                extra = jnp.where(wide % 64 < 32, extra_re, extra_im)
                result += jnp.where((wide < 64) == (g == 0), extra, 0.0)
                inner[pl.ds(b + 2 * pair + e, HALF, stride=HALF), :] = result
    picked_ref[...] = inner[(HALF - 8) * HALF : (HALF - 6) * HALF]


def rows_kernel(place_ref, picked_ref, picked2_ref, rows_ref):
    first = place_ref[0] == 0
    for e in range(2):
        at = slice(e * HALF, (e + 1) * HALF)
        value = jnp.concatenate([picked_ref[at], picked2_ref[at]], axis=0)
        shape = (64, 64)
        mixed = (lax.broadcasted_iota(jnp.int32, shape, 0) < HALF) != (lanes_of(shape) < HALF)
        for part in range(2):
            one = jnp.concatenate(
                [value[:, part * 32 : part * 32 + 32], value[:, 64 + part * 32 : 96 + part * 32]], axis=1
            )
            one = one - jnp.where(mixed, one, 0.0).T
            top = jnp.where(first, one[0:HALF], one[HALF:64])
            low = jnp.where(first, one[HALF:64], one[0:HALF])
            both = jnp.concatenate([top, low], axis=0)
            left, right = both[:, 0:HALF], both[:, HALF:64]
            rows_ref[e, part] = jnp.concatenate(
                [jnp.where(first, left, right), jnp.where(first, right, left)], axis=1
            )


def correlate_kernel(place_ref, flipped_ref, full_ref, inner_ref, inner2_ref, sink_ref, corr_ref):
    run = place_ref[1]
    combos = flipped_ref.shape[0]
    shape = (STEPS, 128)
    step = lax.broadcasted_iota(jnp.int32, shape, 0)
    share = jnp.where(lanes_of(shape) < 64, 1.0 / 3.0, 1.0) * jnp.where(step == STEPS - 1, 0.5, 1.0)
    sink = []
    for e in range(2):
        shape = (HALF, STEPS)
        target = (2 * run + e + lanes_of(shape) + 1) % HALF
        move = jnp.where(lax.broadcasted_iota(jnp.int32, shape, 0) == target, 1.0, 0.0).astype(BF16)
        high, low = split(sink_ref[e * STEPS : (e + 1) * STEPS] * share)
        placed = dot_nn(move, high) + dot_nn(move, low)
        for part in range(2):
            one = jnp.concatenate(
                [placed[:, part * 32 : part * 32 + 32], placed[:, 64 + part * 32 : 96 + part * 32]], axis=1
            )
            one = jnp.concatenate([one, jnp.zeros((HALF, 64), F32)], axis=0)
            sink.append(one - one.T)
    sink_high, sink_low = split(jnp.concatenate(sink, axis=1))
    sink_stack = jnp.concatenate([sink_high, sink_low, sink_high], axis=0)

    shape = (128, 128)
    row, lane = lax.broadcasted_iota(jnp.int32, shape, 0), lanes_of(shape)
    cross = (row < 64) != (lane < 64)
    side = jnp.where(lanes_of((64, 128)) < 64, 1.0, -1.0)
    results = []
    for s in range(combos):
        dual = []
        whole = dot_nn(flipped_ref[s], sink_stack)
        for q in range(3):
            out = whole[q * 128 : (q + 1) * 128]
            re = jnp.concatenate([out[0:32], out[64:96]], axis=0)
            im = jnp.concatenate([out[32:64], out[96:128]], axis=0)
            per_row = []
            for e in range(2):
                re_e, im_e = re[:, e * 128 : (e + 1) * 128], im[:, e * 128 : (e + 1) * 128]
                per_row.append(
                    (
                        re_e + pltpu.roll(im_e, 64, 1) * side,
                        im_e - pltpu.roll(re_e, 64, 1) * side,
                    )
                )
            dual.append(per_row)
        blocks = []
        for slot in range(3):
            at = slice((s * 6 + slot * 2) * HALF, (s * 6 + slot * 2 + 2) * HALF)
            blocks.append(jnp.concatenate([inner_ref[at], inner2_ref[at]], axis=0))
        masked = [jnp.where(cross, block, 0.0) for block in blocks]
        acc_re, acc_im = jnp.zeros((HALF, 128), F32), jnp.zeros((HALF, 128), F32)
        for q, lefts, partners in (
            (2, (blocks[0], blocks[1]), (0, 1)),
            (1, (blocks[2], masked[1]), (0, 2)),
            (0, (masked[0], masked[2]), (2, 1)),
        ):
            high, low = split(jnp.concatenate(lefts, axis=0))
            out = dot_nt(jnp.concatenate([high, low], axis=1), full_ref[s * 3 + q])
            out = out[:, 0:128] + out[:, 128:256]
            for k in range(2):
                for g in range(2):
                    for e in range(2):
                        at = k * 128 + g * 64 + e * HALF
                        part = out[at : at + HALF]
                        half = slice(g * HALF, (g + 1) * HALF)
                        acc_re += part * dual[partners[k]][e][0][half]
                        acc_im += part * dual[partners[k]][e][1][half]
        results.append((jnp.sum(acc_re, axis=0, keepdims=True), jnp.sum(acc_im, axis=0, keepdims=True)))
    shape = (combos, 128)
    diagonal = lax.broadcasted_iota(jnp.int32, shape, 0) == lanes_of(shape)
    both = []
    for part in range(2):
        table = jnp.sum(jnp.concatenate([result[part] for result in results], axis=0), axis=1, keepdims=True)
        both.append(jnp.sum(jnp.where(diagonal, table, 0.0), axis=0, keepdims=True))
    corr_ref[...] = jnp.broadcast_to(jnp.concatenate(both, axis=0)[None], corr_ref.shape)


def call(kernel, name, outs, ins, scratch, micros, args):
    return pl.pallas_call(
        kernel,
        out_shape=outs,
        in_specs=ins,
        out_specs=jax.tree.map(lambda _: VMEM, outs),
        scratch_shapes=scratch,
        compiler_params=pltpu.CompilerParams(vmem_limit_bytes=6 << 20),
        cost_estimate=pl.CostEstimate(flops=int(micros * 1e9), bytes_accessed=0, transcendentals=0),
        name=name,
    )(*args)


def shape_of(dtype, *dims):
    return jax.ShapeDtypeStruct(dims, dtype)


def prepare(place, choice, peram):
    count = 3 * choice.shape[0]
    return call(
        prepare_kernel,
        "prepare",
        (
            shape_of(BF16, 2, 128, 64),
            shape_of(BF16, 2, 128, 128),
            shape_of(BF16, count // 3, 384, 192),
            shape_of(BF16, count, 256, 256),
        ),
        [SMEM, SMEM, VMEM],
        [pltpu.VMEM((count, 64, 128), F32), pltpu.VMEM((HALF, 128), F32)],
        3,
        (place, choice, peram),
    )


def sum_kernel(parts_ref, own_ref, every_ref):
    own = parts_ref[0]
    for k in range(1, parts_ref.shape[0]):
        own += parts_ref[k]
    own_ref[...] = own
    for k in range(parts_ref.shape[0]):
        every_ref[k] = own


def sum_parts(parts):
    outs = (shape_of(F32, *parts.shape[1:]), shape_of(F32, *parts.shape))
    return call(sum_kernel, "sum_parts", outs, [VMEM], [], 0.2, (parts,))


def first_index(g, left_r, left_n, half):
    scratch = [pltpu.VMEM((HALF * HALF, 128), F32)]
    if g == 1:
        scratch.append(pltpu.VMEM((HALF * STEPS, 128), F32))
    return call(
        functools.partial(first_index_kernel, g),
        "first_index",
        (shape_of(F32, HALF * HALF, 128), shape_of(F32, 2 * HALF, 128)),
        [VMEM] * 3,
        scratch,
        2,
        (left_r, left_n, half),
    )


def own_rows(place, picked):
    return call(rows_kernel, "own_rows", shape_of(F32, 2, 2, 64, 64), [SMEM, VMEM, VMEM], [], 3, (place, *picked))


def correlate(place, flipped, full, inner, sink, copies):
    return call(
        correlate_kernel,
        "correlate",
        shape_of(F32, copies, 2, 128),
        [SMEM] + [VMEM] * 5,
        [],
        3,
        (place, flipped, full, *inner, sink),
    )


def swapped(value, axis, mask):
    count = lax.axis_size(axis)
    return lax.ppermute(value, axis, [(i, i ^ mask) for i in range(count)])


def shards(vectors, perambulators, shift_steps, spin_choice):
    vec = vectors[0]
    nvec = vec.shape[2]
    z_count, run_count = lax.axis_size("z"), lax.axis_size("z") * lax.axis_size("yl")
    space_count = run_count * lax.axis_size("core")
    combos = spin_choice.shape[0]
    factor = 1.0 / math.sqrt(24.0 * vec.shape[3] * space_count)
    corr_factor = 0.25 / (nvec * math.sqrt(nvec))
    core = lax.axis_index("core")
    run = lax.axis_index("z") * lax.axis_size("yl") + lax.axis_index("yl")
    peram = perambulators[0].reshape(-1, 2, nvec, nvec)

    beside = swapped(vec, "core", 1)
    part = pair_products(core[None], vec, factor)
    part = pair_products(core[None], beside, factor, part).reshape(run_count, -1, 128)
    time_count = lax.axis_size("yh") * lax.axis_size("x")
    now = lax.axis_index("yh") * lax.axis_size("x") + lax.axis_index("x")
    away_by = now ^ ((now + shift_steps[0]) % time_count)
    pick = (away_by & 1) * 4 + (away_by & 2) + (away_by >> 2)
    place = jnp.stack([core, run]).astype(jnp.int32)
    place, pick, part = lax.optimization_barrier((place, pick, part))
    spread = lax.all_to_all(part, ("z", "yl"), 0, 0, tiled=True)
    left_r, left_n, flipped, full = prepare(place, spin_choice, peram)
    spread, left_r = lax.optimization_barrier((spread, left_r))
    own, every = sum_parts(spread)

    one = swapped(own, "yh", 1)
    near = jnp.stack([own, one])
    two = swapped(near, "x", 2)
    wider = jnp.concatenate([near, two])
    four = swapped(wider, "x", 1)
    mine = lax.all_to_all(every, ("z", "yl"), 0, 0, tiled=True)
    mine, _ = lax.optimization_barrier((mine, two))
    mine = mine.reshape(-1, 128)
    theirs = swapped(mine, "core", 1)
    inner, picked = zip(first_index(0, left_r, left_n, mine), first_index(1, left_r, left_n, theirs), strict=True)
    four, inner = lax.optimization_barrier((four, inner))
    sink = lax.dynamic_index_in_dim(jnp.concatenate([wider, four]), pick, 0, keepdims=False)
    corr = correlate(place, flipped, full, inner, sink, space_count)
    total = lax.all_to_all(corr, ("z", "yl", "core"), 0, 0, tiled=True).sum(0)
    rows = own_rows(place, picked)
    correlator = jnp.transpose((total[:, :combos] * corr_factor)[None], (0, 2, 1))
    return (rows.reshape(1, 2, 2, nvec * nvec)[0], correlator)


def solution(mesh):
    fine = Mesh(mesh.devices.reshape(2, 4, 8, 2, 2), ("yh", "x", "z", "yl", "core"))
    times, space = ("yh", "x"), ("z", "yl", "core")
    placed = (P(times, None, None, None, space), P(times, None, None, None), P(times), P())

    def whole(vectors, perambulators, shift_steps, spin_choice):
        rows, correlator = shards(vectors, perambulators, shift_steps, spin_choice)
        return rows[None], correlator

    return jax.shard_map(
        whole,
        mesh=fine,
        in_specs=placed,
        out_specs=(P(times, space, None, None), P(times, None, None)),
        check_vma=False,
    )
```

time: 71.5 us -> 70.4 us (0.985)
  waiting for transfers between devices: 18.6 us -> 16.6 us
  starting transfers between devices: 30.9 us -> 32.7 us
    all_to_all x1, starting transfers between devices: 6.49 us -> 8.39 us  [shards(): total = lax.all_to_all(corr, ('z', 'yl', 'core'), 0, 0, tiled=True).sum(0)]
    all_to_all x1, waiting for transfers between devices: 2.48 us -> 0.98 us  [shards(): mine = lax.all_to_all(every, ('z', 'yl'), 0, 0, tiled=True)]
    unnamed x8 -> x10, local copies, waits for them, and re-layouts: 1.05 us -> 1.89 us
    all_to_all x1, waiting for transfers between devices: 6.56 us -> 5.77 us  [shards(): spread = lax.all_to_all(part, ('z', 'yl'), 0, 0, tiled=True)]
    add x1 -> x0, other arithmetic: 0.75 us -> none  [shards(): part = (keep + got).reshape(run_count, -1, 128)]
    broadcast_in_dim x1 -> x0, local copies, waits for them, and re-layouts: 0.74 us -> none  [shards(): every = jnp.broadcast_to(own[None], (run_count,) + own.shape)]
    pallas_call x4 -> x6, Pallas kernels: 11.3 us -> 10.8 us  [call(): pl.pallas_call(kernel, out_shape=outs, in_specs=ins, out_specs=jax.tree.m...]
  transfers between devices with their start and end apart: 8 -> 8, of which waited for: 5 -> 5; matrix products, arithmetic and copies ran while one was open for 2% -> 2% of each run, Pallas kernels for 15% -> 13%
where the time goes in v4:
time: 70.4 us; the launch traced here: 70 us
  starting transfers between devices  32.7 us (46%)
  waiting for transfers between devices  16.6 us (24%)
  Pallas kernels  15.2 us (22%)
  local copies, waits for them, and re-layouts  3.26 us (5%)
  between operations  1.46 us (2%)
  other arithmetic  0.72 us (1%)
    ppermute x5, starting transfers between devices, swapped(): return lax.ppermute(value, axis, [(i, i ^ mask) for i in range(count)])  13.3 us
    pallas_call x6, Pallas kernels, call(): pl.pallas_call(kernel, out_shape=outs, in_specs=ins, out_specs=jax.tree.m...  10.8 us
    all_to_all x1, starting transfers between devices, shards(): total = lax.all_to_all(corr, ('z', 'yl', 'core'), 0, 0, tiled=True).sum(0)  8.39 us
    all_to_all x1, starting transfers between devices, shards(): spread = lax.all_to_all(part, ('z', 'yl'), 0, 0, tiled=True)  7.57 us
    all_to_all x1, waiting for transfers between devices, shards(): total = lax.all_to_all(corr, ('z', 'yl', 'core'), 0, 0, tiled=True).sum(0)  6.46 us
    all_to_all x1, waiting for transfers between devices, shards(): spread = lax.all_to_all(part, ('z', 'yl'), 0, 0, tiled=True)  5.77 us
    pallas_call x2, Pallas kernels, pair_products(): pl.pallas_call(functools.partial(pair_kernel, factor), out_shape=jax.Shap...  4.37 us
    all_to_all x1, starting transfers between devices, shards(): mine = lax.all_to_all(every, ('z', 'yl'), 0, 0, tiled=True)  3.53 us
  transfers between devices with their start and end apart: 8, of which 5 were waited for; matrix products, arithmetic and copies ran while one was open for 2% of the time, Pallas kernels for 13%

profile of v4, /device:TPU:1, one launch (start us, length us, event | category | flops | bytes accessed | tf_op | source)
XLA Modules:
  0.0 70.0 jit_solution(12045691565805143947)
XLA Ops:
  0.6 3.3 %collective-permute-start = (f32[2,3,64,256]{3,2,1,0:T(8,128)}, f32[2,3,64,256]{3,2,1,0:T(8,128)S(1)}, u32[]{:S(2)}, u32[]{:S(2)}) collective-permute-start(f32[2,3,64,256]{3,2,1,0:T(8,128)} %bitcast.17), channel_id=1, source_target_pairs={{0,1},{1,0},{2,3},{3,2},{4,5},{5,4},{6,7},{7,6},{8,9},{9,8},{10,11... | collective-permute-start | bytes 1179656 | tf_op jit(solution)/shard_map/ppermute | solution.py:436
  4.6 1.0 %copy-done = f32[1,2,3,64,256]{4,3,2,1,0:T(8,128)S(1)} copy-done((f32[1,2,3,64,256]{4,3,2,1,0:T(8,128)S(1)}, f32[1,2,3,64,256]{4,3,2,1,0:T(8,128)}, u32[]{:S(2)}) %copy-start) | copy-done | bytes 393240
  5.6 1.8 %pair_products.2.refs_0_ = f32[512,128]{1,0:T(8,128)S(1)} custom-call(s32[1]{0:T(128)} %bitcast.half_ref, f32[2,3,64,256]{3,2,1,0:T(8,128)S(1)} %bitcast.18), custom_call_target="tpu_custom_call" | custom-call | tf_op jit(solution)/shard_map/pair_products/pallas_call | solution.py:100
  7.6 2.6 %pair_products.3 = f32[512,128]{1,0:T(8,128)} custom-call(s32[1]{0:T(128)} %bitcast.half_ref, f32[2,3,64,256]{3,2,1,0:T(8,128)S(1)} %collective-permute-done.vec_ref, f32[512,128]{1,0:T(8,128)S(1)} %pair_products.2.refs_0_), custom_call_target="tpu_custom_call" | custom-call | tf_op jit(solution)/shard_map/pair_products/pallas_call | solution.py:100
  10.1 7.6 %all-to-all-start = ((f32[16,32,128]{2,1,0:T(8,128)}), f32[16,32,128]{2,1,0:T(8,128)S(1)}, u32[]{:S(2)}, u32[]{:S(2)}) async-start(f32[16,32,128]{2,1,0:T(8,128)} %bitcast.4), calls=%async_computation | async-start | bytes 524288 | tf_op jit(solution)/shard_map/all_to_all | solution.py:460
  18.3 4.2 %prepare.1 = (bf16[2,128,64]{2,1,0:T(8,128)(2,1)S(1)}, bf16[2,128,128]{2,1,0:T(8,128)(2,1)S(1)}, bf16[4,384,192]{2,1,0:T(8,128)(2,1)S(1)}, bf16[12,256,256]{2,1,0:T(8,128)(2,1)S(1)}) custom-call(s32[2]{0:T(128)S(1)} %pad_add_fusion.place_ref, s32[4,3]{1,0:T(4,128)S(1)} %copy-done.1, f32[16,2,64,64]{3,2,1,0:T(8,128)S(1)} %reshape_squeeze.3.peram_ref), custom_call_target="tpu_custom_call" | custom-call | flops 3000000000 | tf_op jit(solution)/shard_map/prepare/pallas_call | solution.py:355
  22.5 0.9 %copy-done.2 = bf16[4,384,192]{2,1,0:T(8,128)(2,1)} copy-done((bf16[4,384,192]{2,1,0:T(8,128)(2,1)}, bf16[4,384,192]{2,1,0:T(8,128)(2,1)S(1)}, u32[]{:S(2)}) %copy-start.2) | copy-done | bytes 589848
  23.4 5.8 %all-to-all-done.parts_ref = f32[16,32,128]{2,1,0:T(8,128)S(1)} async-done(((f32[16,32,128]{2,1,0:T(8,128)}), f32[16,32,128]{2,1,0:T(8,128)S(1)}, u32[]{:S(2)}, u32[]{:S(2)}) %all-to-all-start) | async-done | bytes 262176 | tf_op jit(solution)/shard_map/all_to_all | solution.py:460
  29.2 0.8 %sum_parts.1 = (f32[32,128]{1,0:T(8,128)S(1)}, f32[16,32,128]{2,1,0:T(8,128)}) custom-call(f32[16,32,128]{2,1,0:T(8,128)S(1)} %all-to-all-done.parts_ref), custom_call_target="tpu_custom_call" | custom-call | flops 200000000 | tf_op jit(solution)/shard_map/sum_parts/pallas_call | solution.py:355
  29.9 3.5 %all-to-all-start.1 = ((f32[16,32,128]{2,1,0:T(8,128)}), f32[16,32,128]{2,1,0:T(8,128)S(1)}, u32[]{:S(2)}, u32[]{:S(2)}) async-start(f32[16,32,128]{2,1,0:T(8,128)} %get-tuple-element.27), calls=%async_computation.1 | async-start | bytes 524288 | tf_op jit(solution)/shard_map/all_to_all | solution.py:470
  33.5 2.7 %collective-permute-start.1 = (f32[32,128]{1,0:T(8,128)S(1)}, f32[32,128]{1,0:T(8,128)S(1)}, u32[]{:S(2)}, u32[]{:S(2)}) collective-permute-start(f32[32,128]{1,0:T(8,128)S(1)} %get-tuple-element.28), channel_id=1, source_target_pairs={{0,128},{128,0},{1,129},{129,1},{2,130},{130,2},{3,131},{131,3},{4... | collective-permute-start | bytes 49160 | tf_op jit(solution)/shard_map/ppermute | solution.py:436
  36.2 1.5 %collective-permute-done.1 = f32[32,128]{1,0:T(8,128)S(1)} collective-permute-done((f32[32,128]{1,0:T(8,128)S(1)}, f32[32,128]{1,0:T(8,128)S(1)}, u32[]{:S(2)}, u32[]{:S(2)}) %collective-permute-start.1) | collective-permute-done | bytes 16416 | tf_op jit(solution)/shard_map/ppermute | solution.py:436
  37.7 2.7 %collective-permute-start.2 = (f32[2,32,128]{2,1,0:T(8,128)S(1)}, f32[2,32,128]{2,1,0:T(8,128)S(1)}, u32[]{:S(2)}, u32[]{:S(2)}) collective-permute-start(f32[2,32,128]{2,1,0:T(8,128)S(1)} %pad_maximum_fusion.1), channel_id=1, source_target_pairs={{0,64},{32,96},{64,0},{96,32},{1,65},{33,97},{65,1},{97,33},{2,66}... | collective-permute-start | bytes 98312 | tf_op jit(solution)/shard_map/ppermute | solution.py:436
  40.4 1.8 %collective-permute-done.2 = f32[2,32,128]{2,1,0:T(8,128)S(1)} collective-permute-done((f32[2,32,128]{2,1,0:T(8,128)S(1)}, f32[2,32,128]{2,1,0:T(8,128)S(1)}, u32[]{:S(2)}, u32[]{:S(2)}) %collective-permute-start.2) | collective-permute-done | bytes 32800 | tf_op jit(solution)/shard_map/ppermute | solution.py:436
  42.2 1.0 %all-to-all-done.1 = f32[16,32,128]{2,1,0:T(8,128)S(1)} async-done(((f32[16,32,128]{2,1,0:T(8,128)}), f32[16,32,128]{2,1,0:T(8,128)S(1)}, u32[]{:S(2)}, u32[]{:S(2)}) %all-to-all-start.1) | async-done | bytes 262176 | tf_op jit(solution)/shard_map/all_to_all | solution.py:470
  43.2 3.3 %collective-permute-start.3 = (f32[512,128]{1,0:T(8,128)S(1)}, f32[512,128]{1,0:T(8,128)S(1)}, u32[]{:S(2)}, u32[]{:S(2)}) collective-permute-start(f32[512,128]{1,0:T(8,128)S(1)} %bitcast.19), channel_id=1, source_target_pairs={{0,1},{1,0},{2,3},{3,2},{4,5},{5,4},{6,7},{7,6},{8,9},{9,8},{10,11... | collective-permute-start | bytes 786440 | tf_op jit(solution)/shard_map/ppermute | solution.py:436
  46.5 1.2 %collective-permute-start.4 = (f32[4,32,128]{2,1,0:T(8,128)S(1)}, f32[4,32,128]{2,1,0:T(8,128)S(1)}, u32[]{:S(2)}, u32[]{:S(2)}) collective-permute-start(f32[4,32,128]{2,1,0:T(8,128)S(1)} %pad_maximum_fusion), channel_id=1, source_target_pairs={{0,32},{32,0},{64,96},{96,64},{1,33},{33,1},{65,97},{97,65},{2,34}... | collective-permute-start | bytes 196616 | tf_op jit(solution)/shard_map/ppermute | solution.py:436
  47.7 1.1 %first_index.2 = (f32[1024,128]{1,0:T(8,128)S(1)}, f32[64,128]{1,0:T(8,128)S(1)}) custom-call(bf16[2,128,64]{2,1,0:T(8,128)(2,1)S(1)} %get-tuple-element.24.left_r_ref, bf16[2,128,128]{2,1,0:T(8,128)(2,1)S(1)} %get-tuple-element.25.left_n_ref, f32[512,128]{1,0:T(8,128)S(1)} %bitcast.20), custom_call_target="tpu_custom_call" | custom-call | flops 2000000000 | tf_op jit(solution)/shard_map/first_index/pallas_call | solution.py:355
  48.9 1.3 %first_index.3 = (f32[1024,128]{1,0:T(8,128)S(1)}, f32[64,128]{1,0:T(8,128)S(1)}) custom-call(bf16[2,128,64]{2,1,0:T(8,128)(2,1)S(1)} %get-tuple-element.24.left_r_ref, bf16[2,128,128]{2,1,0:T(8,128)(2,1)S(1)} %get-tuple-element.25.left_n_ref, f32[512,128]{1,0:T(8,128)S(1)} %collective-permute-done.3.from_ref), custom_call_target="tpu_custom_call" | custom-call | flops 2000000000 | tf_op jit(solution)/shard_map/first_index/pallas_call | solution.py:355
  50.2 2.6 %correlate.1 = f32[32,2,128]{2,1,0:T(2,128)} custom-call(s32[2]{0:T(128)S(1)} %pad_add_fusion.place_ref, bf16[4,384,192]{2,1,0:T(8,128)(2,1)S(1)} %copy-done.3, bf16[12,256,256]{2,1,0:T(8,128)(2,1)S(1)} %get-tuple-element.33.full_ref, f32[1024,128]{1,0:T(8,128)S(1)} %get-tuple-element.36.inner_ref, f32[1024,128]{1,0:T(8,128)S(1)} %get-tuple-element.37.inner2_ref, ...), custom_call_target="tpu_custom_call" | custom-call | flops 3000000000 | tf_op jit(solution)/shard_map/correlate/pallas_call | solution.py:355
  52.8 8.4 %all-to-all-start.2 = ((f32[32,2,128]{2,1,0:T(2,128)}), f32[32,2,128]{2,1,0:T(2,128)S(1)}, u32[]{:S(2)}, u32[]{:S(2)}) async-start(f32[32,2,128]{2,1,0:T(2,128)} %correlate.1), calls=%async_computation.2 | async-start | bytes 65536 | tf_op jit(solution)/shard_map/all_to_all | solution.py:478
  61.2 0.9 %own_rows.1 = f32[2,2,64,64]{3,2,1,0:T(8,128)S(1)} custom-call(s32[2]{0:T(128)S(1)} %pad_add_fusion.place_ref, f32[64,128]{1,0:T(8,128)S(1)} %get-tuple-element.30.picked_ref, f32[64,128]{1,0:T(8,128)S(1)} %get-tuple-element.31.picked2_ref), custom_call_target="tpu_custom_call" | custom-call | flops 3000000000 | tf_op jit(solution)/shard_map/own_rows/pallas_call | solution.py:355
  62.1 0.7 %broadcast_in_dim_squeeze_reshape.3 = f32[1,2,2,4096]{3,2,1,0:T(2,128)} reshape(f32[2,2,64,64]{3,2,1,0:T(8,128)S(1)} %own_rows.1) | data formatting | bytes 131072 | tf_op jit(solution)/shard_map/broadcast_in_dim;squeeze;reshape | solution.py:491
  62.9 6.5 %all-to-all-done.2 = f32[32,2,128]{2,1,0:T(2,128)S(1)} async-done(((f32[32,2,128]{2,1,0:T(2,128)}), f32[32,2,128]{2,1,0:T(2,128)S(1)}, u32[]{:S(2)}, u32[]{:S(2)}) %all-to-all-start.2) | async-done | bytes 32800 | tf_op jit(solution)/shard_map/all_to_all | solution.py:478
  (18 shorter events, 1.4 us)
Async XLA Ops:
  0.6 6.9 %collective-permute-start = (f32[2,3,64,256]{3,2,1,0:T(8,128)}, f32[2,3,64,256]{3,2,1,0:T(8,128)S(1)}, u32[]{:S(2)}, u32[]{:S(2)}) collective-permute-start(f32[2,3,64,256]{3,2,1,0:T(8,128)} %bitcast.17), channel_id=1, source_target_pairs={{0,1},{1,0},{2,3},{3,2},{4,5},{5,4},{6,7},{7,6},{8,9},{9,8},{10,11... | collective-permute-start | bytes 1179656 | tf_op jit(solution)/shard_map/ppermute | solution.py:436
  4.6 1.0 %copy-start = (f32[1,2,3,64,256]{4,3,2,1,0:T(8,128)S(1)}, f32[1,2,3,64,256]{4,3,2,1,0:T(8,128)}, u32[]{:S(2)}) copy-start(f32[1,2,3,64,256]{4,3,2,1,0:T(8,128)} %param.4) | copy-start | bytes 1179652
  5.6 12.1 %copy-start.4 = (f32[1,16,2,4096]{3,2,1,0:T(2,128)S(1)}, f32[1,16,2,4096]{3,2,1,0:T(2,128)}, u32[]{:S(2)}) copy-start(f32[1,16,2,4096]{3,2,1,0:T(2,128)} %param.5) | copy-start | bytes 1572868
  7.5 10.9 %copy-start.1 = (s32[4,3]{1,0:T(4,128)S(1)}, s32[4,3]{1,0:T(4,128)}, u32[]{:S(2)}) copy-start(s32[4,3]{1,0:T(4,128)} %choice_ref.1) | copy-start | bytes 148
  10.1 19.1 %all-to-all-start = ((f32[16,32,128]{2,1,0:T(8,128)}), f32[16,32,128]{2,1,0:T(8,128)S(1)}, u32[]{:S(2)}, u32[]{:S(2)}) async-start(f32[16,32,128]{2,1,0:T(8,128)} %bitcast.4), calls=%async_computation | async-start | bytes 524288 | tf_op jit(solution)/shard_map/all_to_all | solution.py:460
  22.5 0.9 %copy-start.2 = (bf16[4,384,192]{2,1,0:T(8,128)(2,1)}, bf16[4,384,192]{2,1,0:T(8,128)(2,1)S(1)}, u32[]{:S(2)}) copy-start(bf16[4,384,192]{2,1,0:T(8,128)(2,1)S(1)} %get-tuple-element.32.flipped_ref) | copy-start | bytes 1769476
  29.9 13.3 %all-to-all-start.1 = ((f32[16,32,128]{2,1,0:T(8,128)}), f32[16,32,128]{2,1,0:T(8,128)S(1)}, u32[]{:S(2)}, u32[]{:S(2)}) async-start(f32[16,32,128]{2,1,0:T(8,128)} %get-tuple-element.27), calls=%async_computation.1 | async-start | bytes 524288 | tf_op jit(solution)/shard_map/all_to_all | solution.py:470
  33.5 4.2 %collective-permute-start.1 = (f32[32,128]{1,0:T(8,128)S(1)}, f32[32,128]{1,0:T(8,128)S(1)}, u32[]{:S(2)}, u32[]{:S(2)}) collective-permute-start(f32[32,128]{1,0:T(8,128)S(1)} %get-tuple-element.28), channel_id=1, source_target_pairs={{0,128},{128,0},{1,129},{129,1},{2,130},{130,2},{3,131},{131,3},{4... | collective-permute-start | bytes 49160 | tf_op jit(solution)/shard_map/ppermute | solution.py:436
  37.7 4.6 %collective-permute-start.2 = (f32[2,32,128]{2,1,0:T(8,128)S(1)}, f32[2,32,128]{2,1,0:T(8,128)S(1)}, u32[]{:S(2)}, u32[]{:S(2)}) collective-permute-start(f32[2,32,128]{2,1,0:T(8,128)S(1)} %pad_maximum_fusion.1), channel_id=1, source_target_pairs={{0,64},{32,96},{64,0},{96,32},{1,65},{33,97},{65,1},{97,33},{2,66}... | collective-permute-start | bytes 98312 | tf_op jit(solution)/shard_map/ppermute | solution.py:436
  43.2 5.6 %collective-permute-start.3 = (f32[512,128]{1,0:T(8,128)S(1)}, f32[512,128]{1,0:T(8,128)S(1)}, u32[]{:S(2)}, u32[]{:S(2)}) collective-permute-start(f32[512,128]{1,0:T(8,128)S(1)} %bitcast.19), channel_id=1, source_target_pairs={{0,1},{1,0},{2,3},{3,2},{4,5},{5,4},{6,7},{7,6},{8,9},{9,8},{10,11... | collective-permute-start | bytes 786440 | tf_op jit(solution)/shard_map/ppermute | solution.py:436
  46.5 3.6 %collective-permute-start.4 = (f32[4,32,128]{2,1,0:T(8,128)S(1)}, f32[4,32,128]{2,1,0:T(8,128)S(1)}, u32[]{:S(2)}, u32[]{:S(2)}) collective-permute-start(f32[4,32,128]{2,1,0:T(8,128)S(1)} %pad_maximum_fusion), channel_id=1, source_target_pairs={{0,32},{32,0},{64,96},{96,64},{1,33},{33,1},{65,97},{97,65},{2,34}... | collective-permute-start | bytes 196616 | tf_op jit(solution)/shard_map/ppermute | solution.py:436
  48.8 1.3 %copy-start.3 = (bf16[4,384,192]{2,1,0:T(8,128)(2,1)S(1)}, bf16[4,384,192]{2,1,0:T(8,128)(2,1)}, u32[]{:S(2)}) copy-start(bf16[4,384,192]{2,1,0:T(8,128)(2,1)} %copy-done.2) | copy-start | bytes 1769476
  52.8 16.5 %all-to-all-start.2 = ((f32[32,2,128]{2,1,0:T(2,128)}), f32[32,2,128]{2,1,0:T(2,128)S(1)}, u32[]{:S(2)}, u32[]{:S(2)}) async-start(f32[32,2,128]{2,1,0:T(2,128)} %correlate.1), calls=%async_computation.2 | async-start | bytes 65536 | tf_op jit(solution)/shard_map/all_to_all | solution.py:478

commit v5 on v4

--- a/solution.py
+++ b/solution.py
@@ -468,7 +468,6 @@
     wider = jnp.concatenate([near, two])
     four = swapped(wider, "x", 1)
     mine = lax.all_to_all(every, ("z", "yl"), 0, 0, tiled=True)
-    mine, _ = lax.optimization_barrier((mine, two))
     mine = mine.reshape(-1, 128)
     theirs = swapped(mine, "core", 1)
     inner, picked = zip(first_index(0, left_r, left_n, mine), first_index(1, left_r, left_n, theirs), strict=True)

time: 70.4 us -> 70.1 us (level)
    all_to_all x1, waiting for transfers between devices: 0.98 us -> 2.83 us  [shards(): mine = lax.all_to_all(every, ('z', 'yl'), 0, 0, tiled=True)]
    ppermute x5, waiting for transfers between devices: 3.35 us -> 1.63 us  [swapped(): return lax.ppermute(value, axis, [(i, i ^ mask) for i in range(count)])]
where the time goes in v5:
time: 70.1 us; the launch traced here: 69.7 us
  starting transfers between devices  32.4 us (46%)
  waiting for transfers between devices  16.7 us (24%)
  Pallas kernels  15.2 us (22%)
  local copies, waits for them, and re-layouts  3.26 us (5%)
  between operations  1.45 us (2%)
  other arithmetic  0.71 us (1%)
    ppermute x5, starting transfers between devices, swapped(): return lax.ppermute(value, axis, [(i, i ^ mask) for i in range(count)])  13.5 us
    pallas_call x6, Pallas kernels, call(): pl.pallas_call(kernel, out_shape=outs, in_specs=ins, out_specs=jax.tree.m...  10.8 us
    all_to_all x1, starting transfers between devices, shards(): total = lax.all_to_all(corr, ('z', 'yl', 'core'), 0, 0, tiled=True).sum(0)  7.74 us
    all_to_all x1, starting transfers between devices, shards(): spread = lax.all_to_all(part, ('z', 'yl'), 0, 0, tiled=True)  7.57 us
    all_to_all x1, waiting for transfers between devices, shards(): total = lax.all_to_all(corr, ('z', 'yl', 'core'), 0, 0, tiled=True).sum(0)  6.46 us
    all_to_all x1, waiting for transfers between devices, shards(): spread = lax.all_to_all(part, ('z', 'yl'), 0, 0, tiled=True)  5.77 us
    pallas_call x2, Pallas kernels, pair_products(): pl.pallas_call(functools.partial(pair_kernel, factor), out_shape=jax.Shap...  4.37 us
    all_to_all x1, starting transfers between devices, shards(): mine = lax.all_to_all(every, ('z', 'yl'), 0, 0, tiled=True)  3.53 us
  transfers between devices with their start and end apart: 8, of which 5 were waited for; matrix products, arithmetic and copies ran while one was open for 2% of the time, Pallas kernels for 13%

profile of v5, /device:TPU:1, one launch (start us, length us, event | category | flops | bytes accessed | tf_op | source)
XLA Modules:
  0.0 69.7 jit_solution(1679345822165031732)
XLA Ops:
  0.6 3.3 %collective-permute-start = (f32[2,3,64,256]{3,2,1,0:T(8,128)}, f32[2,3,64,256]{3,2,1,0:T(8,128)S(1)}, u32[]{:S(2)}, u32[]{:S(2)}) collective-permute-start(f32[2,3,64,256]{3,2,1,0:T(8,128)} %bitcast.17), channel_id=1, source_target_pairs={{0,1},{1,0},{2,3},{3,2},{4,5},{5,4},{6,7},{7,6},{8,9},{9,8},{10,11... | collective-permute-start | bytes 1179656 | tf_op jit(solution)/shard_map/ppermute | solution.py:436
  4.6 1.0 %copy-done = f32[1,2,3,64,256]{4,3,2,1,0:T(8,128)S(1)} copy-done((f32[1,2,3,64,256]{4,3,2,1,0:T(8,128)S(1)}, f32[1,2,3,64,256]{4,3,2,1,0:T(8,128)}, u32[]{:S(2)}) %copy-start) | copy-done | bytes 393240
  5.6 1.8 %pair_products.2.refs_0_ = f32[512,128]{1,0:T(8,128)S(1)} custom-call(s32[1]{0:T(128)} %bitcast.half_ref, f32[2,3,64,256]{3,2,1,0:T(8,128)S(1)} %bitcast.18), custom_call_target="tpu_custom_call" | custom-call | tf_op jit(solution)/shard_map/pair_products/pallas_call | solution.py:100
  7.6 2.6 %pair_products.3 = f32[512,128]{1,0:T(8,128)} custom-call(s32[1]{0:T(128)} %bitcast.half_ref, f32[2,3,64,256]{3,2,1,0:T(8,128)S(1)} %collective-permute-done.vec_ref, f32[512,128]{1,0:T(8,128)S(1)} %pair_products.2.refs_0_), custom_call_target="tpu_custom_call" | custom-call | tf_op jit(solution)/shard_map/pair_products/pallas_call | solution.py:100
  10.1 7.6 %all-to-all-start = ((f32[16,32,128]{2,1,0:T(8,128)}), f32[16,32,128]{2,1,0:T(8,128)S(1)}, u32[]{:S(2)}, u32[]{:S(2)}) async-start(f32[16,32,128]{2,1,0:T(8,128)} %bitcast.4), calls=%async_computation | async-start | bytes 524288 | tf_op jit(solution)/shard_map/all_to_all | solution.py:460
  17.7 0.6 reshape_squeeze.3.peram_ref
  18.3 4.2 %prepare.1 = (bf16[2,128,64]{2,1,0:T(8,128)(2,1)S(1)}, bf16[2,128,128]{2,1,0:T(8,128)(2,1)S(1)}, bf16[4,384,192]{2,1,0:T(8,128)(2,1)S(1)}, bf16[12,256,256]{2,1,0:T(8,128)(2,1)S(1)}) custom-call(s32[2]{0:T(128)S(1)} %pad_add_fusion.place_ref, s32[4,3]{1,0:T(4,128)S(1)} %copy-done.1, f32[16,2,64,64]{3,2,1,0:T(8,128)S(1)} %reshape_squeeze.3.peram_ref), custom_call_target="tpu_custom_call" | custom-call | flops 3000000000 | tf_op jit(solution)/shard_map/prepare/pallas_call | solution.py:355
  22.5 0.9 %copy-done.2 = bf16[4,384,192]{2,1,0:T(8,128)(2,1)} copy-done((bf16[4,384,192]{2,1,0:T(8,128)(2,1)}, bf16[4,384,192]{2,1,0:T(8,128)(2,1)S(1)}, u32[]{:S(2)}) %copy-start.2) | copy-done | bytes 589848
  23.4 5.8 %all-to-all-done.parts_ref = f32[16,32,128]{2,1,0:T(8,128)S(1)} async-done(((f32[16,32,128]{2,1,0:T(8,128)}), f32[16,32,128]{2,1,0:T(8,128)S(1)}, u32[]{:S(2)}, u32[]{:S(2)}) %all-to-all-start) | async-done | bytes 262176 | tf_op jit(solution)/shard_map/all_to_all | solution.py:460
  29.2 0.8 %sum_parts.1 = (f32[32,128]{1,0:T(8,128)S(1)}, f32[16,32,128]{2,1,0:T(8,128)}) custom-call(f32[16,32,128]{2,1,0:T(8,128)S(1)} %all-to-all-done.parts_ref), custom_call_target="tpu_custom_call" | custom-call | flops 200000000 | tf_op jit(solution)/shard_map/sum_parts/pallas_call | solution.py:355
  29.9 3.5 %all-to-all-start.1 = ((f32[16,32,128]{2,1,0:T(8,128)}), f32[16,32,128]{2,1,0:T(8,128)S(1)}, u32[]{:S(2)}, u32[]{:S(2)}) async-start(f32[16,32,128]{2,1,0:T(8,128)} %get-tuple-element.26), calls=%async_computation.1 | async-start | bytes 524288 | tf_op jit(solution)/shard_map/all_to_all | solution.py:470
  33.5 2.7 %collective-permute-start.2 = (f32[32,128]{1,0:T(8,128)S(1)}, f32[32,128]{1,0:T(8,128)S(1)}, u32[]{:S(2)}, u32[]{:S(2)}) collective-permute-start(f32[32,128]{1,0:T(8,128)S(1)} %get-tuple-element.31), channel_id=1, source_target_pairs={{0,128},{128,0},{1,129},{129,1},{2,130},{130,2},{3,131},{131,3},{4... | collective-permute-start | bytes 49160 | tf_op jit(solution)/shard_map/ppermute | solution.py:436
  36.2 1.5 %collective-permute-done.2 = f32[32,128]{1,0:T(8,128)S(1)} collective-permute-done((f32[32,128]{1,0:T(8,128)S(1)}, f32[32,128]{1,0:T(8,128)S(1)}, u32[]{:S(2)}, u32[]{:S(2)}) %collective-permute-start.2) | collective-permute-done | bytes 16416 | tf_op jit(solution)/shard_map/ppermute | solution.py:436
  37.7 2.7 %collective-permute-start.3 = (f32[2,32,128]{2,1,0:T(8,128)S(1)}, f32[2,32,128]{2,1,0:T(8,128)S(1)}, u32[]{:S(2)}, u32[]{:S(2)}) collective-permute-start(f32[2,32,128]{2,1,0:T(8,128)S(1)} %pad_maximum_fusion.1), channel_id=1, source_target_pairs={{0,64},{32,96},{64,0},{96,32},{1,65},{33,97},{65,1},{97,33},{2,66}... | collective-permute-start | bytes 98312 | tf_op jit(solution)/shard_map/ppermute | solution.py:436
  40.4 2.8 %all-to-all-done.1 = f32[16,32,128]{2,1,0:T(8,128)S(1)} async-done(((f32[16,32,128]{2,1,0:T(8,128)}), f32[16,32,128]{2,1,0:T(8,128)S(1)}, u32[]{:S(2)}, u32[]{:S(2)}) %all-to-all-start.1) | async-done | bytes 262176 | tf_op jit(solution)/shard_map/all_to_all | solution.py:470
  43.2 3.3 %collective-permute-start.1 = (f32[512,128]{1,0:T(8,128)S(1)}, f32[512,128]{1,0:T(8,128)S(1)}, u32[]{:S(2)}, u32[]{:S(2)}) collective-permute-start(f32[512,128]{1,0:T(8,128)S(1)} %bitcast.19), channel_id=1, source_target_pairs={{0,1},{1,0},{2,3},{3,2},{4,5},{5,4},{6,7},{7,6},{8,9},{9,8},{10,11... | collective-permute-start | bytes 786440 | tf_op jit(solution)/shard_map/ppermute | solution.py:436
  46.5 1.5 %collective-permute-start.4 = (f32[4,32,128]{2,1,0:T(8,128)S(1)}, f32[4,32,128]{2,1,0:T(8,128)S(1)}, u32[]{:S(2)}, u32[]{:S(2)}) collective-permute-start(f32[4,32,128]{2,1,0:T(8,128)S(1)} %pad_maximum_fusion), channel_id=1, source_target_pairs={{0,32},{32,0},{64,96},{96,64},{1,33},{33,1},{65,97},{97,65},{2,34}... | collective-permute-start | bytes 196616 | tf_op jit(solution)/shard_map/ppermute | solution.py:436
  48.0 1.1 %first_index.2 = (f32[1024,128]{1,0:T(8,128)S(1)}, f32[64,128]{1,0:T(8,128)S(1)}) custom-call(bf16[2,128,64]{2,1,0:T(8,128)(2,1)S(1)} %get-tuple-element.23.left_r_ref, bf16[2,128,128]{2,1,0:T(8,128)(2,1)S(1)} %get-tuple-element.24.left_n_ref, f32[512,128]{1,0:T(8,128)S(1)} %bitcast.20), custom_call_target="tpu_custom_call" | custom-call | flops 2000000000 | tf_op jit(solution)/shard_map/first_index/pallas_call | solution.py:355
  49.1 1.3 %first_index.3 = (f32[1024,128]{1,0:T(8,128)S(1)}, f32[64,128]{1,0:T(8,128)S(1)}) custom-call(bf16[2,128,64]{2,1,0:T(8,128)(2,1)S(1)} %get-tuple-element.23.left_r_ref, bf16[2,128,128]{2,1,0:T(8,128)(2,1)S(1)} %get-tuple-element.24.left_n_ref, f32[512,128]{1,0:T(8,128)S(1)} %collective-permute-done.1.from_ref), custom_call_target="tpu_custom_call" | custom-call | flops 2000000000 | tf_op jit(solution)/shard_map/first_index/pallas_call | solution.py:355
  50.6 2.6 %correlate.1 = f32[32,2,128]{2,1,0:T(2,128)} custom-call(s32[2]{0:T(128)S(1)} %pad_add_fusion.place_ref, bf16[4,384,192]{2,1,0:T(8,128)(2,1)S(1)} %copy-done.3, bf16[12,256,256]{2,1,0:T(8,128)(2,1)S(1)} %get-tuple-element.30.full_ref, f32[1024,128]{1,0:T(8,128)S(1)} %get-tuple-element.34.inner_ref, f32[1024,128]{1,0:T(8,128)S(1)} %get-tuple-element.35.inner2_ref, ...), custom_call_target="tpu_custom_call" | custom-call | flops 3000000000 | tf_op jit(solution)/shard_map/correlate/pallas_call | solution.py:355
  53.2 7.7 %all-to-all-start.2 = ((f32[32,2,128]{2,1,0:T(2,128)}), f32[32,2,128]{2,1,0:T(2,128)S(1)}, u32[]{:S(2)}, u32[]{:S(2)}) async-start(f32[32,2,128]{2,1,0:T(2,128)} %correlate.1), calls=%async_computation.2 | async-start | bytes 65536 | tf_op jit(solution)/shard_map/all_to_all | solution.py:477
  60.9 0.9 %own_rows.1 = f32[2,2,64,64]{3,2,1,0:T(8,128)S(1)} custom-call(s32[2]{0:T(128)S(1)} %pad_add_fusion.place_ref, f32[64,128]{1,0:T(8,128)S(1)} %get-tuple-element.27.picked_ref, f32[64,128]{1,0:T(8,128)S(1)} %get-tuple-element.28.picked2_ref), custom_call_target="tpu_custom_call" | custom-call | flops 3000000000 | tf_op jit(solution)/shard_map/own_rows/pallas_call | solution.py:355
  61.9 0.7 %broadcast_in_dim_squeeze_reshape.3 = f32[1,2,2,4096]{3,2,1,0:T(2,128)} reshape(f32[2,2,64,64]{3,2,1,0:T(8,128)S(1)} %own_rows.1) | data formatting | bytes 131072 | tf_op jit(solution)/shard_map/broadcast_in_dim;squeeze;reshape | solution.py:490
  62.6 6.5 %all-to-all-done.2 = f32[32,2,128]{2,1,0:T(2,128)S(1)} async-done(((f32[32,2,128]{2,1,0:T(2,128)}), f32[32,2,128]{2,1,0:T(2,128)S(1)}, u32[]{:S(2)}, u32[]{:S(2)}) %all-to-all-start.2) | async-done | bytes 32800 | tf_op jit(solution)/shard_map/all_to_all | solution.py:477
  (18 shorter events, 0.9 us)
Async XLA Ops:
  0.6 6.9 %collective-permute-start = (f32[2,3,64,256]{3,2,1,0:T(8,128)}, f32[2,3,64,256]{3,2,1,0:T(8,128)S(1)}, u32[]{:S(2)}, u32[]{:S(2)}) collective-permute-start(f32[2,3,64,256]{3,2,1,0:T(8,128)} %bitcast.17), channel_id=1, source_target_pairs={{0,1},{1,0},{2,3},{3,2},{4,5},{5,4},{6,7},{7,6},{8,9},{9,8},{10,11... | collective-permute-start | bytes 1179656 | tf_op jit(solution)/shard_map/ppermute | solution.py:436
  4.6 1.0 %copy-start = (f32[1,2,3,64,256]{4,3,2,1,0:T(8,128)S(1)}, f32[1,2,3,64,256]{4,3,2,1,0:T(8,128)}, u32[]{:S(2)}) copy-start(f32[1,2,3,64,256]{4,3,2,1,0:T(8,128)} %param.4) | copy-start | bytes 1179652
  5.6 12.1 %copy-start.4 = (f32[1,16,2,4096]{3,2,1,0:T(2,128)S(1)}, f32[1,16,2,4096]{3,2,1,0:T(2,128)}, u32[]{:S(2)}) copy-start(f32[1,16,2,4096]{3,2,1,0:T(2,128)} %param.5) | copy-start | bytes 1572868
  7.5 10.9 %copy-start.1 = (s32[4,3]{1,0:T(4,128)S(1)}, s32[4,3]{1,0:T(4,128)}, u32[]{:S(2)}) copy-start(s32[4,3]{1,0:T(4,128)} %choice_ref.1) | copy-start | bytes 148
  10.1 19.1 %all-to-all-start = ((f32[16,32,128]{2,1,0:T(8,128)}), f32[16,32,128]{2,1,0:T(8,128)S(1)}, u32[]{:S(2)}, u32[]{:S(2)}) async-start(f32[16,32,128]{2,1,0:T(8,128)} %bitcast.4), calls=%async_computation | async-start | bytes 524288 | tf_op jit(solution)/shard_map/all_to_all | solution.py:460
  22.5 0.9 %copy-start.2 = (bf16[4,384,192]{2,1,0:T(8,128)(2,1)}, bf16[4,384,192]{2,1,0:T(8,128)(2,1)S(1)}, u32[]{:S(2)}) copy-start(bf16[4,384,192]{2,1,0:T(8,128)(2,1)S(1)} %get-tuple-element.29.flipped_ref) | copy-start | bytes 1769476
  29.9 13.3 %all-to-all-start.1 = ((f32[16,32,128]{2,1,0:T(8,128)}), f32[16,32,128]{2,1,0:T(8,128)S(1)}, u32[]{:S(2)}, u32[]{:S(2)}) async-start(f32[16,32,128]{2,1,0:T(8,128)} %get-tuple-element.26), calls=%async_computation.1 | async-start | bytes 524288 | tf_op jit(solution)/shard_map/all_to_all | solution.py:470
  33.5 4.2 %collective-permute-start.2 = (f32[32,128]{1,0:T(8,128)S(1)}, f32[32,128]{1,0:T(8,128)S(1)}, u32[]{:S(2)}, u32[]{:S(2)}) collective-permute-start(f32[32,128]{1,0:T(8,128)S(1)} %get-tuple-element.31), channel_id=1, source_target_pairs={{0,128},{128,0},{1,129},{129,1},{2,130},{130,2},{3,131},{131,3},{4... | collective-permute-start | bytes 49160 | tf_op jit(solution)/shard_map/ppermute | solution.py:436
  37.7 8.9 %collective-permute-start.3 = (f32[2,32,128]{2,1,0:T(8,128)S(1)}, f32[2,32,128]{2,1,0:T(8,128)S(1)}, u32[]{:S(2)}, u32[]{:S(2)}) collective-permute-start(f32[2,32,128]{2,1,0:T(8,128)S(1)} %pad_maximum_fusion.1), channel_id=1, source_target_pairs={{0,64},{32,96},{64,0},{96,32},{1,65},{33,97},{65,1},{97,33},{2,66}... | collective-permute-start | bytes 98312 | tf_op jit(solution)/shard_map/ppermute | solution.py:436
  43.2 5.9 %collective-permute-start.1 = (f32[512,128]{1,0:T(8,128)S(1)}, f32[512,128]{1,0:T(8,128)S(1)}, u32[]{:S(2)}, u32[]{:S(2)}) collective-permute-start(f32[512,128]{1,0:T(8,128)S(1)} %bitcast.19), channel_id=1, source_target_pairs={{0,1},{1,0},{2,3},{3,2},{4,5},{5,4},{6,7},{7,6},{8,9},{9,8},{10,11... | collective-permute-start | bytes 786440 | tf_op jit(solution)/shard_map/ppermute | solution.py:436
  46.5 4.0 %collective-permute-start.4 = (f32[4,32,128]{2,1,0:T(8,128)S(1)}, f32[4,32,128]{2,1,0:T(8,128)S(1)}, u32[]{:S(2)}, u32[]{:S(2)}) collective-permute-start(f32[4,32,128]{2,1,0:T(8,128)S(1)} %pad_maximum_fusion), channel_id=1, source_target_pairs={{0,32},{32,0},{64,96},{96,64},{1,33},{33,1},{65,97},{97,65},{2,34}... | collective-permute-start | bytes 196616 | tf_op jit(solution)/shard_map/ppermute | solution.py:436
  49.1 1.4 %copy-start.3 = (bf16[4,384,192]{2,1,0:T(8,128)(2,1)S(1)}, bf16[4,384,192]{2,1,0:T(8,128)(2,1)}, u32[]{:S(2)}) copy-start(bf16[4,384,192]{2,1,0:T(8,128)(2,1)} %copy-done.2) | copy-start | bytes 1769476
  53.2 15.9 %all-to-all-start.2 = ((f32[32,2,128]{2,1,0:T(2,128)}), f32[32,2,128]{2,1,0:T(2,128)S(1)}, u32[]{:S(2)}, u32[]{:S(2)}) async-start(f32[32,2,128]{2,1,0:T(2,128)} %correlate.1), calls=%async_computation.2 | async-start | bytes 65536 | tf_op jit(solution)/shard_map/all_to_all | solution.py:477
